TPU v7x, 128 devices: a whole 4x4x4 slice. The times are simulated.
128 devices in a mesh: row: 4 (over y), col: 32 (over z, x, core).
Axes of the slice: x: 4, y: 4, z: 4, core: 2. Of those that a mesh axis runs over, the one named last changes fastest.
Arguments:
- row_points: bfloat16 [98304, 64], P(('row', 'col')), as said below
- col_points: bfloat16 [32768, 64], P('col'), as said below
- row_logmass: bfloat16 [98304], P(('row', 'col')), may hold values from -4 to 4
- col_logmass: float32 [32768], P('col'), may hold values from -4 to 4
- col_potential: float32 [32768], P('col'), may hold values from -3 to 11
Outputs:
- row_potential: float32 [98304], P('row')
- new_col_potential: float32 [32768], P('col')
Inputs may be any that keep to these rules, and one draw needn't show every extreme that they name: `row_points`: latent coordinates. `col_points`: latent coordinates.
All inputs are finite; a program needn't handle non-finite values.
Results may differ from a plain program's by a relative error of at most 0.0008.
Values may be sent and summed in bfloat16 or wider, within the bound.
No kernel may reach another device: no remote copies, remote signals or barrier semaphores. Data moves between devices by JAX's collectives and lax.ppermute only.
A program may use at most 64 MiB of HBM per device.

v0:
```python
import functools

import jax
import jax.numpy as jnp
from jax import lax
from jax.experimental import pallas as pl
from jax.experimental.pallas import tpu as pltpu
from jax.sharding import Mesh
from jax.sharding import PartitionSpec as P

epsilon = 0.05
dim = 64
rows_own = 768
cols_own = 1024
ring = 4
depth = 80
ln2 = 0.6931471805599453
kappa = 40.0 / ln2
margin = 80.0
chunk = 256
careful = 64
finite_max = 3.0e38
sampled = 64
row_lines = rows_own // 128
offsets = (0, 1, 3, 2)


def split3(v):
    first = v.astype(jnp.bfloat16)
    rest = v - first.astype(jnp.float32)
    second = rest.astype(jnp.bfloat16)
    third = (rest - second.astype(jnp.float32)).astype(jnp.bfloat16)
    return [p.astype(jnp.float32) for p in (first, second, third)]


def place(rows, width):
    index = lax.broadcasted_iota(jnp.int32, (16, width), 0)
    block = jnp.zeros((16, width), jnp.float32)
    for at, row in enumerate(rows):
        block = jnp.where(index == at, jnp.broadcast_to(row, (16, width)), block)
    return block.astype(jnp.bfloat16)


def turned(tile):
    pad = jnp.zeros((128 - depth, 128), jnp.bfloat16)
    return jnp.concatenate([tile, pad], axis=0).T


def score(left, right):
    return lax.dot_general(
        left, right, (((1,), (0,)), ((), ())), preferred_element_type=jnp.float32
    )


def sampled_shift(left, right):
    sample = score(left[0:sampled, 0:depth], right)
    return kappa * jnp.max(sample, axis=0, keepdims=True) + margin


def shifted_sum(left, right, shift, count):
    width = right.shape[1]
    acc = jnp.zeros((8, width), jnp.float32)
    for u in range(count // chunk):
        s = score(left[u * chunk:(u + 1) * chunk, 0:depth], right)
        p = jnp.exp2(s * kappa - shift)
        acc = acc + jnp.sum(p.reshape(chunk // 8, 8, width), axis=0)
    return jnp.sum(acc, axis=0, keepdims=True)


def exact_log(lefts, right):
    width = right.shape[1]
    peak = jnp.full((1, width), -finite_max, jnp.float32)
    total = jnp.zeros((1, width), jnp.float32)

    def rows_at(left, u):
        return left[pl.ds(pl.multiple_of(u * careful, careful), careful), 0:depth]

    for left in lefts:
        def peak_step(u, peak, left=left):
            return jnp.maximum(peak, jnp.max(score(rows_at(left, u), right), axis=0, keepdims=True))

        peak = lax.fori_loop(0, left.shape[0] // careful, peak_step, peak)
    for left in lefts:
        def sum_step(u, total, left=left):
            s = score(rows_at(left, u), right)
            return total + jnp.sum(jnp.exp2((s - peak) * kappa), axis=0, keepdims=True)

        total = lax.fori_loop(0, left.shape[0] // careful, sum_step, total)
    return kappa * peak + jnp.log2(total)


def prepare_kernel(y, pot, logmass, cols_out):
    one = jnp.ones((1, cols_own), jnp.float32)
    yw = y[...].astype(jnp.float32)
    norm = jnp.sum(yw * yw, axis=0, keepdims=True)
    c = 0.5 * (pot[...] - norm) + (0.5 * epsilon) * logmass[...]
    cols_out[0:dim, :] = y[...]
    cols_out[dim:depth, :] = place(split3(c) + [one, one, one], cols_own)


def to_lines(line):
    count = line.shape[1] // 128
    parts = [line[:, t * 128:(t + 1) * 128] for t in range(count)]
    if count < 8:
        parts.append(jnp.zeros((8 - count, 128), jnp.float32))
    return jnp.concatenate(parts, axis=0)


def eight(at):
    return pl.ds(pl.multiple_of(at * 8, 8), 8)


def log_add(*terms):
    peak = terms[0]
    for t in terms[1:]:
        peak = jnp.maximum(peak, t)
    total = jnp.exp2(terms[0] - peak)
    for t in terms[1:]:
        total = total + jnp.exp2(t - peak)
    return peak + jnp.log2(total)


def line_of(lines, count):
    return jnp.concatenate([lines[t:t + 1, :] for t in range(count)], axis=1)


def forward_kernel(n_rows, n_cols, n_turned, n_old, n_mass, *refs):
    refs = list(refs)
    take = lambda n: [refs.pop(0) for _ in range(n)]
    rows, cols, lefts, olds, mass = take(n_rows), take(n_cols), take(n_turned), take(n_old), take(n_mass)
    out = refs.pop(0)
    stack = refs.pop(-1)
    if cols:
        ys = refs.pop(0)
        for q, col in enumerate(cols):
            def turn(t, carry, q=q, col=col):
                at = pl.multiple_of(t * 128, 128)
                ys[pl.ds(pl.multiple_of(q * cols_own + at, 128), 128), :] = turned(col[:, pl.ds(at, 128)])
                return carry

            lax.fori_loop(0, cols_own // 128, turn, 0, unroll=4)
        lefts = lefts + [ys]
    one = jnp.ones((1, rows_own), jnp.float32)
    extras = place([one, one, one], rows_own)
    for b, row in enumerate(rows):
        stack[b, 0:dim, :] = row[...]
        stack[b, dim:depth, :] = extras
    at = 0
    for old in olds:
        out[at:at + old.shape[0], :] = old[...]
        at += old.shape[0]

    def block(b, worst):
        right = stack[b]
        if olds:
            shift = line_of(out[eight(b), :], row_lines) + margin
            total = 2.0 ** -margin
        else:
            shift = sampled_shift(lefts[0], right)
            total = 0.0
        for left in lefts:
            total = total + shifted_sum(left, right, shift, left.shape[0])
        logs = shift + jnp.log2(total)
        out[eight(b), :] = to_lines(logs)
        return jnp.maximum(worst, logs)

    worst = lax.fori_loop(0, n_rows, block, jnp.full((1, rows_own), -finite_max, jnp.float32))

    @pl.when(jnp.logical_not(jnp.max(worst) < finite_max))
    def _():
        at = 0
        for old in olds:
            out[at:at + old.shape[0], :] = old[...]
            at += old.shape[0]

        def exact(b, carry):
            logs = to_lines(exact_log(lefts, stack[b]))
            out[eight(b), :] = log_add(out[eight(b), :], logs) if olds else logs
            return carry

        lax.fori_loop(0, n_rows, exact, 0)

    if mass:
        out[ring * 8:(ring + 1) * 8, :] = to_lines(mass[0][...].astype(jnp.float32))


def merge_rows_kernel(place_x, own, far1, far3, far2, x0, x1, x3, x2, potential, ready):
    fars, points = (own, far1, far3, far2), (x0, x1, x3, x2)
    one = jnp.ones((1, rows_own), jnp.float32)
    found = []
    for b in range(ring):
        lines = [(b ^ d) * 8 for d in range(ring)]
        merged = log_add(*[far[n:n + row_lines, :] for n, far in zip(lines, fars)])
        mass = fars[b][ring * 8:ring * 8 + row_lines, :]
        xw = points[b][...].astype(jnp.float32)
        norm = jnp.sum(xw * xw, axis=0, keepdims=True)
        norm = jnp.concatenate([norm[:, t * 128:(t + 1) * 128] for t in range(row_lines)], axis=0)
        found.append(norm - (epsilon * ln2) * merged)
        r = mass * (0.5 * epsilon) - merged * (1.0 / kappa)
        tall = jnp.concatenate(
            [points[b][...], place([one, one, one] + split3(line_of(r, row_lines)), rows_own)], axis=0
        )
        for t in range(row_lines):
            at = b * rows_own + t * 128
            ready[at:at + 128, :] = turned(tall[:, t * 128:(t + 1) * 128])
    x = place_x[0]
    for index in range(ring):
        value = found[offsets.index(index)]
        for other in range(1, ring):
            value = jnp.where(x == other, found[offsets.index(index ^ other)], value)
        potential[index * row_lines:(index + 1) * row_lines, :] = value


def column_logs(xs, cols, logs, stack):
    for q, col in enumerate(cols):
        stack[q] = col[...]

    def block(q, worst):
        right = stack[q]
        shift = sampled_shift(xs, right)
        found = shift + jnp.log2(shifted_sum(xs, right, shift, ring * rows_own))
        logs[eight(q), :] = to_lines(found)
        return jnp.maximum(worst, found)

    worst = lax.fori_loop(0, len(cols), block, jnp.full((1, cols_own), -finite_max, jnp.float32))

    @pl.when(jnp.logical_not(jnp.max(worst) < finite_max))
    def _():
        def exact(q, carry):
            logs[eight(q), :] = to_lines(exact_log([xs], stack[q]))
            return carry

        lax.fori_loop(0, len(cols), exact, 0)


def backward_kernel(xs, *refs):
    column_logs(xs, refs[:-2], refs[-2], refs[-1])


def to_core_kernel(logs, potential, out):
    out[0:32, :] = logs[...]
    out[32:56, :] = potential[...]


def backward_last_kernel(place_z, xs, c3, c2, early, swapped, out, logs, stack):
    column_logs(xs, (c3, c2), logs, stack)
    for p, d in enumerate(offsets):
        mine = (early if p < 2 else logs)[p % 2 * 8:(p % 2 + 1) * 8, :]
        value = log_add(mine, swapped[p * 8:(p + 1) * 8, :])
        for y in range(ring):
            out[y * ring + (place_z[0] ^ d)] = value


def pack_kernel(core, mine, theirs, out):
    first = core[0] == 0
    for x in range(ring):
        a = mine[32 + x * row_lines:32 + (x + 1) * row_lines, :]
        b = theirs[32 + x * row_lines:32 + (x + 1) * row_lines, :]
        at = 2 * x * row_lines
        out[at:at + row_lines, :] = jnp.where(first, a, b)
        out[at + row_lines:at + 2 * row_lines, :] = jnp.where(first, b, a)


def pack_two_kernel(mine, far, out):
    out[0:48, :] = mine[...]
    out[48:96, :] = far[...]


def final_kernel(place_z, parts, pot, logmass, mine, near, out, potential):
    merged = log_add(*[parts[i] for i in range(ring * ring)])
    out[...] = pot[...] + epsilon * logmass[...] - (epsilon * ln2) * merged
    z = place_z[0]
    for other, ref, at in ((0, mine, 0), (3, mine, 48), (1, near, 0), (2, near, 48)):
        potential[pl.ds(pl.multiple_of((z ^ other) * 48, 8), 48), :] = ref[at:at + 48, :]


def call(kernel, name, out, args, mib=24, pairs=0, scratch=(), scalars=0, last=False):
    within = {} if last else {"out_specs": jax.tree.map(lambda _: pl.BlockSpec(memory_space=pltpu.VMEM), out)}
    specs = [pl.BlockSpec(memory_space=pltpu.SMEM)] * scalars
    specs += [pl.BlockSpec(memory_space=pltpu.VMEM)] * (len(args) - scalars)
    return pl.pallas_call(
        kernel,
        out_shape=out,
        in_specs=specs,
        **within,
        scratch_shapes=list(scratch),
        compiler_params=pltpu.CompilerParams(vmem_limit_bytes=mib << 20),
        cost_estimate=pl.CostEstimate(flops=pairs * 512, bytes_accessed=1 << 20, transcendentals=pairs),
        name=name,
    )(*args)


def across(value, axis, bits):
    return lax.ppermute(value, axis, [(i, i ^ bits) for i in range(ring)])


def swap(value):
    return lax.ppermute(value, "k", [(0, 1), (1, 0)])


def after(value, *earlier):
    return lax.optimization_barrier((value, *earlier))[0]


def shape(*dims, dtype=jnp.float32):
    return jax.ShapeDtypeStruct(dims, dtype)


def index_of(axis):
    return lax.axis_index(axis).astype(jnp.int32).reshape(1)


def stack_of(count, *dims):
    return pltpu.VMEM((count, depth, *dims), jnp.bfloat16)


def forward(rows, cols=(), lefts=(), olds=(), mass=()):
    outs = [shape(8 * len(rows) + (8 if mass else 0), 128)]
    turned_cols = (len(cols) * cols_own, 128)
    scratch = [pltpu.VMEM(turned_cols, jnp.bfloat16)] if mass else []
    if cols and not mass:
        outs.append(shape(*turned_cols, dtype=jnp.bfloat16))
    kernel = functools.partial(forward_kernel, len(rows), len(cols), len(lefts), len(olds), len(mass))
    pairs = len(rows) * rows_own * (len(cols) + 2 * len(lefts)) * cols_own
    return call(
        kernel, "forward", tuple(outs), (*rows, *cols, *lefts, *olds, *mass), pairs=pairs,
        scratch=scratch + [stack_of(len(rows), rows_own)],
    )


def body(row_points, col_points, row_logmass, col_logmass, col_potential):
    mass_r = row_logmass.reshape(1, rows_own)
    mine = row_points.T
    x1, x3 = (across(mine, "x", d) for d in (1, 3))
    own = call(
        prepare_kernel, "prepare", shape(depth, cols_own, dtype=jnp.bfloat16),
        (col_points.T, col_potential.reshape(1, cols_own), col_logmass.reshape(1, cols_own)),
    )
    z1, z3 = (across(own, "z", d) for d in (1, 3))
    over0 = swap(own)
    some = (mine, x1, x3)
    logs, ys0 = forward(some, (own, over0))
    x2 = across(after(x1, logs), "x", 3)
    z2 = across(after(z1, logs), "z", 3)
    over1, over3 = swap(after(z1, logs)), swap(after(z3, logs))
    logs, ys1 = forward(some, (z1, z3), olds=(logs,))
    over1, over3, _ = lax.optimization_barrier((over1, over3, logs))
    logs, ys2 = forward(some, (over1, over3), olds=(logs,))
    x2 = after(x2, logs)
    logs2 = forward((x2,), lefts=(ys0, ys1, ys2))[0]
    over2 = swap(after(z2, logs))
    over2 = after(over2, logs2)
    logs = forward((*some, x2), (z2, over2), olds=(logs, logs2), mass=(mass_r,))[0]

    fars = [across(logs, "x", d) for d in (1, 3, 2)]
    potential, ready = call(
        merge_rows_kernel, "merge_rows",
        (shape(ring * row_lines, 128), shape(ring * rows_own, 128, dtype=jnp.bfloat16)),
        (index_of("x"), logs, *fars, *some, x2), scalars=1,
    )

    block = ring * rows_own * cols_own
    other = call(
        backward_kernel, "backward", shape(32, 128), (ready, over0, over1, over3, over2), pairs=4 * block,
        scratch=[stack_of(4, cols_own)],
    )
    to_core = call(to_core_kernel, "to_core", shape(56, 128), (other, potential))
    swapped = swap(to_core)
    early = call(backward_kernel, "backward", shape(16, 128), (after(ready, to_core), own, z1), pairs=2 * block, scratch=[stack_of(2, cols_own)])
    swapped = after(swapped, early)
    chip = call(pack_kernel, "pack", shape(48, 128), (index_of("k"), to_core, swapped), scalars=1)
    far = across(chip, "z", 3)
    sums = call(
        backward_last_kernel, "backward_last", shape(ring * ring, 8, 128),
        (index_of("z"), ready, z3, z2, early, swapped),
        pairs=2 * block, scratch=[pltpu.VMEM((16, 128), jnp.float32), stack_of(2, cols_own)], scalars=1,
    )
    parts = lax.all_to_all(sums, ("y", "z"), 0, 0)
    chips = call(pack_two_kernel, "pack_two", shape(96, 128), (chip, after(far, sums)))
    new_col, row_potential = call(
        final_kernel, "finish", (shape(8, 128), shape(ring * 48, 128)),
        (index_of("z"), parts, col_potential.reshape(8, 128), col_logmass.reshape(8, 128),
         chips, across(chips, "z", 1)), scalars=1, last=True,
    )
    return row_potential.reshape(-1), new_col.reshape(cols_own)


def solution(mesh):
    fine = Mesh(mesh.devices.reshape(ring, ring, ring, 2), ("y", "z", "x", "k"))
    cols = ("z", "x", "k")
    every = ("y",) + cols
    return jax.shard_map(
        body,
        mesh=fine,
        in_specs=(P(every, None), P(cols, None), P(every), P(cols), P(cols)),
        out_specs=(P("y"), P(cols)),
        check_vma=False,
    )
```

profile of v0, /device:TPU:0, one launch (start us, length us, event | category | flops | bytes accessed | tf_op | source)
XLA Modules:
  0.0 251.7 jit_solution(9217720904205905169)
XLA Ops:
  0.6 0.0 copy-start.2
  0.6 0.7 copy-done.2
  1.3 0.0 copy-start
  1.3 0.9 copy-done
  2.2 0.0 copy-start.3
  2.2 0.7 copy-done.3
  2.9 0.0 copy-start.1
  2.9 0.0 copy-start.5
  2.9 0.1 prepare.1.refs_3_.refs_0_
  3.0 0.1 collective-permute-start.2
  3.1 0.7 copy-done.1
  3.8 1.6 collective-permute-start
  5.4 2.1 collective-permute-start.1
  7.5 1.9 collective-permute-start.4
  9.4 2.5 %collective-permute-start.6 = (bf16[80,1024]{1,0:T(8,128)(2,1)S(1)}, bf16[80,1024]{1,0:T(8,128)(2,1)S(1)}, u32[]{:S(2)}, u32[]{:S(2)}) collective-permute-start(bf16[80,1024]{1,0:T(8,128)(2,1)S(1)} %prepare.1.refs_3_.refs_0_), channel_id=1, source_target_pairs={{0,24},{8,16},{16,8},{24,0},{1,25},{9,17},{17,9},{25,1},{2,26},{10... | collective-permute-start | bytes 491528 | tf_op jit(solution)/shard_map/ppermute | solution.py:294
  11.9 0.0 copy-done.5
  11.9 0.0 collective-permute-done.refs_1_.x1
  11.9 0.0 collective-permute-done.1.refs_2_.x3
  11.9 0.0 collective-permute-done.2.refs_4_.refs_0_
  12.0 36.8 %forward.5 = (f32[24,128]{1,0:T(8,128)S(1)}, bf16[2048,128]{1,0:T(8,128)(2,1)S(1)}) custom-call(bf16[64,768]{1,0:T(8,128)(2,1)S(1)} %bitcast.14, bf16[64,768]{1,0:T(8,128)(2,1)S(1)} %collective-permute-done.refs_1_.x1, bf16[64,768]{1,0:T(8,128)(2,1)S(1)} %collective-permute-done.1.refs_2_.x3, bf16[80,1024]{1,0:T(8,128)(2,1)S(1)} %prepare.1.refs_3_.refs_0_, ...), custom_call_target="tpu_custom_call" | custom-call | flops 2415919104 | bytes 1048576 | tf_op jit(solution)/shard_map/forward/pallas_call | solution.py:281
  48.7 0.0 collective-permute-done.4.refs_3_.refs_1_
  48.7 0.1 collective-permute-start.5
  48.8 3.4 %collective-permute-start.8 = (bf16[80,1024]{1,0:T(8,128)(2,1)S(1)}, bf16[80,1024]{1,0:T(8,128)(2,1)S(1)}, u32[]{:S(2)}, u32[]{:S(2)}) collective-permute-start(bf16[80,1024]{1,0:T(8,128)(2,1)S(1)} %collective-permute-done.4.refs_3_.refs_1_), channel_id=1, source_target_pairs={{0,24},{8,16},{16,8},{24,0},{1,25},{9,17},{17,9},{25,1},{2,26},{10... | collective-permute-start | bytes 491528 | tf_op jit(solution)/shard_map/ppermute | solution.py:294
  52.2 0.0 collective-permute-done.6.refs_4_.c3
  52.2 0.2 collective-permute-start.7
  52.4 2.1 collective-permute-start.3
  54.5 36.9 %forward.6 = (f32[24,128]{1,0:T(8,128)S(1)}, bf16[2048,128]{1,0:T(8,128)(2,1)S(1)}) custom-call(bf16[64,768]{1,0:T(8,128)(2,1)S(1)} %bitcast.15, bf16[64,768]{1,0:T(8,128)(2,1)S(1)} %collective-permute-done.refs_1_.x1, bf16[64,768]{1,0:T(8,128)(2,1)S(1)} %collective-permute-done.1.refs_2_.x3, bf16[80,1024]{1,0:T(8,128)(2,1)S(1)} %collective-permute-done.4.refs_3_.refs_1_, ...), custom_call_target="tpu_custom_call" | custom-call | flops 2415919104 | bytes 1048576 | tf_op jit(solution)/shard_map/forward/pallas_call | solution.py:281
  91.4 0.0 collective-permute-done.5.refs_3_.refs_1_
  91.4 0.0 collective-permute-done.7.refs_4_.refs_2_
  91.4 36.9 %forward.7 = (f32[24,128]{1,0:T(8,128)S(1)}, bf16[2048,128]{1,0:T(8,128)(2,1)S(1)}) custom-call(bf16[64,768]{1,0:T(8,128)(2,1)S(1)} %bitcast.16, bf16[64,768]{1,0:T(8,128)(2,1)S(1)} %collective-permute-done.refs_1_.x1, bf16[64,768]{1,0:T(8,128)(2,1)S(1)} %collective-permute-done.1.refs_2_.x3, bf16[80,1024]{1,0:T(8,128)(2,1)S(1)} %collective-permute-done.5.refs_3_.refs_1_, ...), custom_call_target="tpu_custom_call" | custom-call | flops 2415919104 | bytes 1048576 | tf_op jit(solution)/shard_map/forward/pallas_call | solution.py:281
  128.3 0.0 collective-permute-done.3.refs_0_.refs_3_.x2
  128.3 0.0 collective-permute-done.8.refs_4_.c2
  128.3 0.1 collective-permute-start.9
  128.5 35.9 %forward.8.refs_7_ = f32[8,128]{1,0:T(8,128)S(1)} custom-call(bf16[64,768]{1,0:T(8,128)(2,1)S(1)} %collective-permute-done.3.refs_0_.refs_3_.x2, bf16[2048,128]{1,0:T(8,128)(2,1)S(1)} %get-tuple-element.33.refs_1_, bf16[2048,128]{1,0:T(8,128)(2,1)S(1)} %get-tuple-element.34.refs_2_, bf16[2048,128]{1,0:T(8,128)(2,1)S(1)} %get-tuple-element.35.refs_3_), custom_call_target="tpu_custom_call" | custom-call | flops 2415919104 | bytes 1048576 | tf_op jit(solution)/shard_map/forward/pallas_call | solution.py:281
  164.4 0.0 collective-permute-done.9.refs_5_.refs_3_
  164.4 48.8 %forward.9.own = f32[40,128]{1,0:T(8,128)S(1)} custom-call(bf16[64,768]{1,0:T(8,128)(2,1)S(1)} %bitcast.17, bf16[64,768]{1,0:T(8,128)(2,1)S(1)} %collective-permute-done.refs_1_.x1, bf16[64,768]{1,0:T(8,128)(2,1)S(1)} %collective-permute-done.1.refs_2_.x3, bf16[64,768]{1,0:T(8,128)(2,1)S(1)} %collective-permute-done.3.refs_0_.refs_3_.x2, ...), custom_call_target="tpu_custom_call" | custom-call | flops 3221225472 | bytes 1048576 | tf_op jit(solution)/shard_map/forward/pallas_call | solution.py:281
  213.2 0.1 collective-permute-start.10
  213.3 1.2 collective-permute-start.11
  214.5 2.9 %collective-permute-start.12 = (f32[40,128]{1,0:T(8,128)S(1)}, f32[40,128]{1,0:T(8,128)S(1)}, u32[]{:S(2)}, u32[]{:S(2)}) collective-permute-start(f32[40,128]{1,0:T(8,128)S(1)} %forward.9.own), channel_id=1, source_target_pairs={{0,4},{2,6},{4,0},{6,2},{1,5},{3,7},{5,1},{7,3},{8,12},{10,14},{12... | collective-permute-start | bytes 61448 | tf_op jit(solution)/shard_map/ppermute | solution.py:294
  217.4 0.0 collective-permute-done.10.far1
  217.4 1.0 collective-permute-done.11.far3
  218.4 1.4 collective-permute-done.12.far2
  219.8 0.3 merge_rows.1
  220.1 7.5 %backward.2.logs = f32[32,128]{1,0:T(8,128)S(1)} custom-call(bf16[3072,128]{1,0:T(8,128)(2,1)S(1)} %get-tuple-element.39.xs, bf16[80,1024]{1,0:T(8,128)(2,1)S(1)} %collective-permute-done.2.refs_4_.refs_0_, bf16[80,1024]{1,0:T(8,128)(2,1)S(1)} %collective-permute-done.5.refs_3_.refs_1_, bf16[80,1024]{1,0:T(8,128)(2,1)S(1)} %collective-permute-done.7.refs_4_.refs_2_, ...), custom_call_target="tpu_custom_call" | custom-call | flops 6442450944 | bytes 1048576 | tf_op jit(solution)/shard_map/backward/pallas_call | solution.py:281
  227.6 0.1 collective-permute-start.13
  227.7 3.8 %backward.3.early = f32[16,128]{1,0:T(8,128)S(1)} custom-call(bf16[3072,128]{1,0:T(8,128)(2,1)S(1)} %get-tuple-element.39.xs, bf16[80,1024]{1,0:T(8,128)(2,1)S(1)} %prepare.1.refs_3_.refs_0_, bf16[80,1024]{1,0:T(8,128)(2,1)S(1)} %collective-permute-done.4.refs_3_.refs_1_), custom_call_target="tpu_custom_call" | custom-call | flops 3221225472 | bytes 1048576 | tf_op jit(solution)/shard_map/backward/pallas_call | solution.py:281
  231.6 0.0 collective-permute-done.13.swapped.theirs
  231.6 0.3 collective-permute-start.14
  231.9 4.5 %backward_last.1 = f32[16,8,128]{2,1,0:T(8,128)} custom-call(s32[1]{0:T(128)} %bitcast.place_z, bf16[3072,128]{1,0:T(8,128)(2,1)S(1)} %get-tuple-element.39.xs, bf16[80,1024]{1,0:T(8,128)(2,1)S(1)} %collective-permute-done.6.refs_4_.c3, bf16[80,1024]{1,0:T(8,128)(2,1)S(1)} %collective-permute-done.8.refs_4_.c2, f32[16,128]{1,0:T(8,128)S(1)} %backward.3.early, ...), custom_call_target="tpu_custom_call" | custom-call | flops 3221225472 | bytes 1048576 | tf_op jit(solution)/shard_map/backward_last/pallas_call | solution.py:281
  236.4 7.0 %all-to-all-start = ((f32[16,8,128]{2,1,0:T(8,128)}), f32[16,8,128]{2,1,0:T(8,128)S(1)}, u32[]{:S(2)}, u32[]{:S(2)}) async-start(f32[16,8,128]{2,1,0:T(8,128)} %backward_last.1), calls=%async_computation | async-start | bytes 131072 | tf_op jit(solution)/shard_map/all_to_all | solution.py:378
  243.4 0.0 collective-permute-done.14.far
  243.4 0.0 copy-start.4
  243.4 2.0 collective-permute-start.15
  245.4 5.6 %all-to-all-done.parts = f32[16,8,128]{2,1,0:T(8,128)S(1)} async-done(((f32[16,8,128]{2,1,0:T(8,128)}), f32[16,8,128]{2,1,0:T(8,128)S(1)}, u32[]{:S(2)}, u32[]{:S(2)}) %all-to-all-start) | async-done | bytes 65568 | tf_op jit(solution)/shard_map/all_to_all | solution.py:378
  251.1 0.0 collective-permute-done.15.near
  251.1 0.0 copy-done.4
  251.1 0.7 finish.1
  (4 shorter events, 0.0 us)
Async XLA Ops:
  0.6 0.7 copy-start.2
  1.3 0.9 copy-start
  2.2 0.7 copy-start.3
  2.9 0.9 copy-start.1
  2.9 9.0 %copy-start.5 = (bf16[768]{0:T(1024)(128)(2,1)S(1)}, bf16[768]{0:T(1024)(128)(2,1)}, u32[]{:S(2)}) copy-start(bf16[768]{0:T(1024)(128)(2,1)} %param.7) | copy-start | bytes 4612
  3.0 9.0 %collective-permute-start.2 = (bf16[80,1024]{1,0:T(8,128)(2,1)S(1)}, bf16[80,1024]{1,0:T(8,128)(2,1)S(1)}, u32[]{:S(2)}, u32[]{:S(2)}) collective-permute-start(bf16[80,1024]{1,0:T(8,128)(2,1)S(1)} %prepare.1.refs_3_.refs_0_), channel_id=1, source_target_pairs={{0,1},{1,0},{2,3},{3,2},{4,5},{5,4},{6,7},{7,6},{8,9},{9,8},{10,11... | collective-permute-start | bytes 491528 | tf_op jit(solution)/shard_map/ppermute | solution.py:298
  3.8 8.1 %collective-permute-start = (bf16[64,768]{1,0:T(8,128)(2,1)S(1)}, bf16[64,768]{1,0:T(8,128)(2,1)S(1)}, u32[]{:S(2)}, u32[]{:S(2)}) collective-permute-start(bf16[64,768]{1,0:T(8,128)(2,1)S(1)} %bitcast.12), channel_id=1, source_target_pairs={{0,2},{2,0},{4,6},{6,4},{1,3},{3,1},{5,7},{7,5},{8,10},{10,8},{12,... | collective-permute-start | bytes 294920 | tf_op jit(solution)/shard_map/ppermute | solution.py:294
  5.4 6.6 %collective-permute-start.1 = (bf16[64,768]{1,0:T(8,128)(2,1)S(1)}, bf16[64,768]{1,0:T(8,128)(2,1)S(1)}, u32[]{:S(2)}, u32[]{:S(2)}) collective-permute-start(bf16[64,768]{1,0:T(8,128)(2,1)S(1)} %bitcast.13), channel_id=1, source_target_pairs={{0,6},{2,4},{4,2},{6,0},{1,7},{3,5},{5,3},{7,1},{8,14},{10,12},{12... | collective-permute-start | bytes 294920 | tf_op jit(solution)/shard_map/ppermute | solution.py:294
  7.5 41.3 %collective-permute-start.4 = (bf16[80,1024]{1,0:T(8,128)(2,1)S(1)}, bf16[80,1024]{1,0:T(8,128)(2,1)S(1)}, u32[]{:S(2)}, u32[]{:S(2)}) collective-permute-start(bf16[80,1024]{1,0:T(8,128)(2,1)S(1)} %prepare.1.refs_3_.refs_0_), channel_id=1, source_target_pairs={{0,8},{8,0},{16,24},{24,16},{1,9},{9,1},{17,25},{25,17},{2,10},{10... | collective-permute-start | bytes 491528 | tf_op jit(solution)/shard_map/ppermute | solution.py:294
  9.4 42.8 %collective-permute-start.6 = (bf16[80,1024]{1,0:T(8,128)(2,1)S(1)}, bf16[80,1024]{1,0:T(8,128)(2,1)S(1)}, u32[]{:S(2)}, u32[]{:S(2)}) collective-permute-start(bf16[80,1024]{1,0:T(8,128)(2,1)S(1)} %prepare.1.refs_3_.refs_0_), channel_id=1, source_target_pairs={{0,24},{8,16},{16,8},{24,0},{1,25},{9,17},{17,9},{25,1},{2,26},{10... | collective-permute-start | bytes 491528 | tf_op jit(solution)/shard_map/ppermute | solution.py:294
  48.7 42.6 %collective-permute-start.5 = (bf16[80,1024]{1,0:T(8,128)(2,1)S(1)}, bf16[80,1024]{1,0:T(8,128)(2,1)S(1)}, u32[]{:S(2)}, u32[]{:S(2)}) collective-permute-start(bf16[80,1024]{1,0:T(8,128)(2,1)S(1)} %collective-permute-done.4.refs_3_.refs_1_), channel_id=1, source_target_pairs={{0,1},{1,0},{2,3},{3,2},{4,5},{5,4},{6,7},{7,6},{8,9},{9,8},{10,11... | collective-permute-start | bytes 491528 | tf_op jit(solution)/shard_map/ppermute | solution.py:298
  48.8 79.5 %collective-permute-start.8 = (bf16[80,1024]{1,0:T(8,128)(2,1)S(1)}, bf16[80,1024]{1,0:T(8,128)(2,1)S(1)}, u32[]{:S(2)}, u32[]{:S(2)}) collective-permute-start(bf16[80,1024]{1,0:T(8,128)(2,1)S(1)} %collective-permute-done.4.refs_3_.refs_1_), channel_id=1, source_target_pairs={{0,24},{8,16},{16,8},{24,0},{1,25},{9,17},{17,9},{25,1},{2,26},{10... | collective-permute-start | bytes 491528 | tf_op jit(solution)/shard_map/ppermute | solution.py:294
  52.2 39.2 %collective-permute-start.7 = (bf16[80,1024]{1,0:T(8,128)(2,1)S(1)}, bf16[80,1024]{1,0:T(8,128)(2,1)S(1)}, u32[]{:S(2)}, u32[]{:S(2)}) collective-permute-start(bf16[80,1024]{1,0:T(8,128)(2,1)S(1)} %collective-permute-done.6.refs_4_.c3), channel_id=1, source_target_pairs={{0,1},{1,0},{2,3},{3,2},{4,5},{5,4},{6,7},{7,6},{8,9},{9,8},{10,11... | collective-permute-start | bytes 491528 | tf_op jit(solution)/shard_map/ppermute | solution.py:298
  52.4 75.9 %collective-permute-start.3 = (bf16[64,768]{1,0:T(8,128)(2,1)S(1)}, bf16[64,768]{1,0:T(8,128)(2,1)S(1)}, u32[]{:S(2)}, u32[]{:S(2)}) collective-permute-start(bf16[64,768]{1,0:T(8,128)(2,1)S(1)} %collective-permute-done.refs_1_.x1), channel_id=1, source_target_pairs={{0,6},{2,4},{4,2},{6,0},{1,7},{3,5},{5,3},{7,1},{8,14},{10,12},{12... | collective-permute-start | bytes 294920 | tf_op jit(solution)/shard_map/ppermute | solution.py:294
  128.3 36.1 %collective-permute-start.9 = (bf16[80,1024]{1,0:T(8,128)(2,1)S(1)}, bf16[80,1024]{1,0:T(8,128)(2,1)S(1)}, u32[]{:S(2)}, u32[]{:S(2)}) collective-permute-start(bf16[80,1024]{1,0:T(8,128)(2,1)S(1)} %collective-permute-done.8.refs_4_.c2), channel_id=1, source_target_pairs={{0,1},{1,0},{2,3},{3,2},{4,5},{5,4},{6,7},{7,6},{8,9},{9,8},{10,11... | collective-permute-start | bytes 491528 | tf_op jit(solution)/shard_map/ppermute | solution.py:298
  213.2 4.2 %collective-permute-start.10 = (f32[40,128]{1,0:T(8,128)S(1)}, f32[40,128]{1,0:T(8,128)S(1)}, u32[]{:S(2)}, u32[]{:S(2)}) collective-permute-start(f32[40,128]{1,0:T(8,128)S(1)} %forward.9.own), channel_id=1, source_target_pairs={{0,2},{2,0},{4,6},{6,4},{1,3},{3,1},{5,7},{7,5},{8,10},{10,8},{12,... | collective-permute-start | bytes 61448 | tf_op jit(solution)/shard_map/ppermute | solution.py:294
  213.3 5.1 %collective-permute-start.11 = (f32[40,128]{1,0:T(8,128)S(1)}, f32[40,128]{1,0:T(8,128)S(1)}, u32[]{:S(2)}, u32[]{:S(2)}) collective-permute-start(f32[40,128]{1,0:T(8,128)S(1)} %forward.9.own), channel_id=1, source_target_pairs={{0,6},{2,4},{4,2},{6,0},{1,7},{3,5},{5,3},{7,1},{8,14},{10,12},{12... | collective-permute-start | bytes 61448 | tf_op jit(solution)/shard_map/ppermute | solution.py:294
  214.5 5.3 %collective-permute-start.12 = (f32[40,128]{1,0:T(8,128)S(1)}, f32[40,128]{1,0:T(8,128)S(1)}, u32[]{:S(2)}, u32[]{:S(2)}) collective-permute-start(f32[40,128]{1,0:T(8,128)S(1)} %forward.9.own), channel_id=1, source_target_pairs={{0,4},{2,6},{4,0},{6,2},{1,5},{3,7},{5,1},{7,3},{8,12},{10,14},{12... | collective-permute-start | bytes 61448 | tf_op jit(solution)/shard_map/ppermute | solution.py:294
  227.6 3.9 %collective-permute-start.13 = (f32[56,128]{1,0:T(8,128)S(1)}, f32[56,128]{1,0:T(8,128)S(1)}, u32[]{:S(2)}, u32[]{:S(2)}) collective-permute-start(f32[56,128]{1,0:T(8,128)S(1)} %to_core.1.mine), channel_id=1, source_target_pairs={{0,1},{1,0},{2,3},{3,2},{4,5},{5,4},{6,7},{7,6},{8,9},{9,8},{10,11... | collective-permute-start | bytes 86024 | tf_op jit(solution)/shard_map/ppermute | solution.py:298
  231.6 11.8 %collective-permute-start.14 = (f32[48,128]{1,0:T(8,128)S(1)}, f32[48,128]{1,0:T(8,128)S(1)}, u32[]{:S(2)}, u32[]{:S(2)}) collective-permute-start(f32[48,128]{1,0:T(8,128)S(1)} %pack.1.mine), channel_id=1, source_target_pairs={{0,24},{8,16},{16,8},{24,0},{1,25},{9,17},{17,9},{25,1},{2,26},{10... | collective-permute-start | bytes 73736 | tf_op jit(solution)/shard_map/ppermute | solution.py:294
  236.4 14.7 %all-to-all-start = ((f32[16,8,128]{2,1,0:T(8,128)}), f32[16,8,128]{2,1,0:T(8,128)S(1)}, u32[]{:S(2)}, u32[]{:S(2)}) async-start(f32[16,8,128]{2,1,0:T(8,128)} %backward_last.1), calls=%async_computation | async-start | bytes 131072 | tf_op jit(solution)/shard_map/all_to_all | solution.py:378
  243.4 7.7 %copy-start.4 = (f32[1024]{0:T(1024)S(1)}, f32[1024]{0:T(1024)}, u32[]{:S(2)}) copy-start(f32[1024]{0:T(1024)} %param.8) | copy-start | bytes 12292
  243.4 7.6 %collective-permute-start.15 = (f32[96,128]{1,0:T(8,128)S(1)}, f32[96,128]{1,0:T(8,128)S(1)}, u32[]{:S(2)}, u32[]{:S(2)}) collective-permute-start(f32[96,128]{1,0:T(8,128)S(1)} %pack_two.1.mine), channel_id=1, source_target_pairs={{0,8},{8,0},{16,24},{24,16},{1,9},{9,1},{17,25},{25,17},{2,10},{10... | collective-permute-start | bytes 147464 | tf_op jit(solution)/shard_map/ppermute | solution.py:294
where the time goes:
time: 252 us
  Pallas kernels  212 us (84%)
  starting transfers between devices  27.6 us (11%)
  waiting for transfers between devices  8.05 us (3%)
  local copies, waits for them, and re-layouts  3.02 us (1%)
    pallas_call x14, Pallas kernels, call(): pl.pallas_call(kernel, out_shape=out, in_specs=specs, **within, scratch_s...  212 us
    ppermute x11, starting transfers between devices, across(): return lax.ppermute(value, axis, [(i, i ^ bits) for i in range(ring)])  20.1 us
    all_to_all x1, starting transfers between devices, body(): parts = lax.all_to_all(sums, ('y', 'z'), 0, 0)  6.99 us
    all_to_all x1, waiting for transfers between devices, body(): parts = lax.all_to_all(sums, ('y', 'z'), 0, 0)  5.63 us
  transfers between devices with their start and end apart: 17, of which 3 were waited for; matrix products, arithmetic and copies ran while one was open for 0% of the time, Pallas kernels for 62%

commit v1 on v0

--- a/solution.py
+++ b/solution.py
@@ -89,13 +89,53 @@
     return kappa * peak + jnp.log2(total)
 
 
-def prepare_kernel(y, pot, logmass, cols_out):
+def prepare_kernel(y_far, pot_far, logmass_far, cols_out, y, pot, logmass, done):
+    copies = [
+        pltpu.make_async_copy(source, target, done.at[i])
+        for i, (source, target) in enumerate(((y_far, y), (pot_far, pot), (logmass_far, logmass)))
+    ]
+    for copy in copies:
+        copy.start()
+    for copy in copies:
+        copy.wait()
     one = jnp.ones((1, cols_own), jnp.float32)
     yw = y[...].astype(jnp.float32)
     norm = jnp.sum(yw * yw, axis=0, keepdims=True)
     c = 0.5 * (pot[...] - norm) + (0.5 * epsilon) * logmass[...]
     cols_out[0:dim, :] = y[...]
     cols_out[dim:depth, :] = place(split3(c) + [one, one, one], cols_own)
+
+
+def pair_kernel(core, mine, theirs, out):
+    out[core[0]] = mine[...]
+    out[1 - core[0]] = theirs[...]
+
+
+def parcel_kernel(core, rows, cols, out):
+    @pl.when(core[0] == 0)
+    def _():
+        out[...] = jnp.zeros(out.shape, jnp.bfloat16)
+        out[:, 0:dim, 0:rows_own] = rows[...]
+
+    @pl.when(core[0] == 1)
+    def _():
+        out[...] = cols[...]
+
+
+def open_kernel(core, here, there, rows, cols):
+    @pl.when(core[0] == 0)
+    def _():
+        rows[...] = here[0, 0:dim, 0:rows_own]
+        cols[...] = there[...]
+
+    @pl.when(core[0] == 1)
+    def _():
+        rows[...] = there[1, 0:dim, 0:rows_own]
+        cols[...] = here[...]
+
+
+def pick_kernel(core, pair, out):
+    out[...] = pair[core[0]]
 
 
 def to_lines(line):
@@ -128,6 +168,8 @@
     refs = list(refs)
     take = lambda n: [refs.pop(0) for _ in range(n)]
     rows, cols, lefts, olds, mass = take(n_rows), take(n_cols), take(n_turned), take(n_old), take(n_mass)
+    if n_cols == 1:
+        cols = [cols[0].at[0], cols[0].at[1]]
     out = refs.pop(0)
     stack = refs.pop(-1)
     if cols:
@@ -164,7 +206,8 @@
         out[eight(b), :] = to_lines(logs)
         return jnp.maximum(worst, logs)
 
-    worst = lax.fori_loop(0, n_rows, block, jnp.full((1, rows_own), -finite_max, jnp.float32))
+    worst = jnp.full((1, rows_own), -finite_max, jnp.float32)
+    worst = lax.fori_loop(0, n_rows, block, worst, unroll=2 if n_rows == ring else 1)
 
     @pl.when(jnp.logical_not(jnp.max(worst) < finite_max))
     def _():
@@ -184,8 +227,11 @@
         out[ring * 8:(ring + 1) * 8, :] = to_lines(mass[0][...].astype(jnp.float32))
 
 
-def merge_rows_kernel(place_x, own, far1, far3, far2, x0, x1, x3, x2, potential, ready):
-    fars, points = (own, far1, far3, far2), (x0, x1, x3, x2)
+def merge_rows_kernel(place_x, core, own, far1, far3, far2, x0, x1, x3, x2, potential, ready):
+    first = core[0] == 0
+    near, far = far1[...], far3[...]
+    fars = (own[...], jnp.where(first, near, far), jnp.where(first, far, near), far2[...])
+    points = (x0, x1, x3, x2)
     one = jnp.ones((1, rows_own), jnp.float32)
     found = []
     for b in range(ring):
@@ -204,6 +250,7 @@
             at = b * rows_own + t * 128
             ready[at:at + 128, :] = turned(tall[:, t * 128:(t + 1) * 128])
     x = place_x[0]
+    found[1], found[2] = jnp.where(first, found[1], found[2]), jnp.where(first, found[2], found[1])
     for index in range(ring):
         value = found[offsets.index(index)]
         for other in range(1, ring):
@@ -211,9 +258,9 @@
         potential[index * row_lines:(index + 1) * row_lines, :] = value
 
 
-def column_logs(xs, cols, logs, stack):
+def column_logs(side, xs, cols, logs, stack):
     for q, col in enumerate(cols):
-        stack[q] = col[...]
+        stack[q] = col[...] if len(col.shape) == 2 else col[side]
 
     def block(q, worst):
         right = stack[q]
@@ -222,7 +269,8 @@
         logs[eight(q), :] = to_lines(found)
         return jnp.maximum(worst, found)
 
-    worst = lax.fori_loop(0, len(cols), block, jnp.full((1, cols_own), -finite_max, jnp.float32))
+    worst = jnp.full((1, cols_own), -finite_max, jnp.float32)
+    worst = lax.fori_loop(0, len(cols), block, worst, unroll=2 if len(cols) > 2 else 1)
 
     @pl.when(jnp.logical_not(jnp.max(worst) < finite_max))
     def _():
@@ -233,8 +281,8 @@
         lax.fori_loop(0, len(cols), exact, 0)
 
 
-def backward_kernel(xs, *refs):
-    column_logs(xs, refs[:-2], refs[-2], refs[-1])
+def backward_kernel(flip, core, xs, *refs):
+    column_logs(core[0] ^ flip, xs, refs[:-2], refs[-2], refs[-1])
 
 
 def to_core_kernel(logs, potential, out):
@@ -242,13 +290,14 @@
     out[32:56, :] = potential[...]
 
 
-def backward_last_kernel(place_z, xs, c3, c2, early, swapped, out, logs, stack):
-    column_logs(xs, (c3, c2), logs, stack)
-    for p, d in enumerate(offsets):
+def backward_last_kernel(place_z, core, xs, c2, c3, early, swapped, out, logs, stack):
+    column_logs(core[0], xs, (c2, c3), logs, stack)
+    bits = (0, 1 + 2 * core[0], 3 - 2 * core[0], 2)
+    for p, other in enumerate((0, 2, 1, 3)):
         mine = (early if p < 2 else logs)[p % 2 * 8:(p % 2 + 1) * 8, :]
-        value = log_add(mine, swapped[p * 8:(p + 1) * 8, :])
+        value = log_add(mine, swapped[other * 8:(other + 1) * 8, :])
         for y in range(ring):
-            out[y * ring + (place_z[0] ^ d)] = value
+            out[y * ring + (place_z[0] ^ bits[p])] = value
 
 
 def pack_kernel(core, mine, theirs, out):
@@ -294,6 +343,11 @@
     return lax.ppermute(value, axis, [(i, i ^ bits) for i in range(ring)])
 
 
+def across_by_core(value, axis, bits0, bits1):
+    pairs = [(2 * i + core, 2 * (i ^ bits) + core) for i in range(ring) for core, bits in enumerate((bits0, bits1))]
+    return lax.ppermute(value, (axis, "k"), pairs)
+
+
 def swap(value):
     return lax.ppermute(value, "k", [(0, 1), (1, 0)])
 
@@ -316,14 +370,15 @@
 
 def forward(rows, cols=(), lefts=(), olds=(), mass=()):
     outs = [shape(8 * len(rows) + (8 if mass else 0), 128)]
-    turned_cols = (len(cols) * cols_own, 128)
+    n_cols = 2 if cols else 0
+    turned_cols = (n_cols * cols_own, 128)
     scratch = [pltpu.VMEM(turned_cols, jnp.bfloat16)] if mass else []
     if cols and not mass:
         outs.append(shape(*turned_cols, dtype=jnp.bfloat16))
     kernel = functools.partial(forward_kernel, len(rows), len(cols), len(lefts), len(olds), len(mass))
-    pairs = len(rows) * rows_own * (len(cols) + 2 * len(lefts)) * cols_own
+    pairs = len(rows) * rows_own * (n_cols + 2 * len(lefts)) * cols_own
     return call(
-        kernel, "forward", tuple(outs), (*rows, *cols, *lefts, *olds, *mass), pairs=pairs,
+        kernel, "forward", tuple(outs), (*rows, *cols, *lefts, *olds, *mass), pairs=pairs // 4,
         scratch=scratch + [stack_of(len(rows), rows_own)],
     )
 
@@ -331,49 +386,86 @@
 def body(row_points, col_points, row_logmass, col_logmass, col_potential):
     mass_r = row_logmass.reshape(1, rows_own)
     mine = row_points.T
-    x1, x3 = (across(mine, "x", d) for d in (1, 3))
-    own = call(
-        prepare_kernel, "prepare", shape(depth, cols_own, dtype=jnp.bfloat16),
-        (col_points.T, col_potential.reshape(1, cols_own), col_logmass.reshape(1, cols_own)),
-    )
-    z1, z3 = (across(own, "z", d) for d in (1, 3))
+    core = index_of("k")
+    bf16 = jnp.bfloat16
+    pair = lambda name, mine, theirs: call(
+        pair_kernel, name, shape(2, *mine.shape, dtype=bf16), (core, mine, theirs), scalars=1
+    )
+    pick = lambda name, value: call(
+        pick_kernel, name, shape(*value.shape[1:], dtype=bf16), (core, value), scalars=1
+    )
+    x_pair = pair("pair_rows", mine, swap(mine))
+    own = pl.pallas_call(
+        prepare_kernel,
+        out_shape=shape(depth, cols_own, dtype=jnp.bfloat16),
+        in_specs=[pl.BlockSpec(memory_space=pltpu.HBM)] * 3,
+        out_specs=pl.BlockSpec(memory_space=pltpu.VMEM),
+        scratch_shapes=[
+            pltpu.VMEM((dim, cols_own), jnp.bfloat16),
+            pltpu.VMEM((1, cols_own), jnp.float32),
+            pltpu.VMEM((1, cols_own), jnp.float32),
+            pltpu.SemaphoreType.DMA((3,)),
+        ],
+        compiler_params=pltpu.CompilerParams(vmem_limit_bytes=60 << 20),
+        name="prepare",
+    )(col_points.T, col_potential.reshape(1, cols_own), col_logmass.reshape(1, cols_own))
     over0 = swap(own)
+    x_near = across_by_core(x_pair, "x", 1, 3)
+    z_near = across_by_core(pair("pair_cols", own, over0), "z", 1, 3)
+    logs, ys0 = forward((mine,), (own, over0))
+    x_near = after(x_near, logs)
+    x_far = swap(x_near)
+    x1 = pick("pick_near", x_near)
+    x3 = pick("pick_far", x_far)
+    logs2 = forward((x1, x3), lefts=(ys0,))[0]
+    z_near = after(z_near, logs2)
+    parcel = call(
+        parcel_kernel, "parcel", shape(2, depth, cols_own, dtype=bf16), (core, x_near, z_near), scalars=1
+    )
+    places = [(z, x, c) for z in range(ring) for x in range(ring) for c in range(2)]
+    number = {place: i for i, place in enumerate(places)}
+    parcel = lax.ppermute(
+        parcel, ("z", "x", "k"),
+        [(i, number[(z, x ^ 3, 0) if c == 0 else (z ^ 1, x, 1)]) for i, (z, x, c) in enumerate(places)],
+    )
+    z_far = swap(z_near)
     some = (mine, x1, x3)
-    logs, ys0 = forward(some, (own, over0))
-    x2 = across(after(x1, logs), "x", 3)
-    z2 = across(after(z1, logs), "z", 3)
-    over1, over3 = swap(after(z1, logs)), swap(after(z3, logs))
-    logs, ys1 = forward(some, (z1, z3), olds=(logs,))
-    over1, over3, _ = lax.optimization_barrier((over1, over3, logs))
-    logs, ys2 = forward(some, (over1, over3), olds=(logs,))
-    x2 = after(x2, logs)
+    logs, ys1 = forward(some, (z_near,), olds=(logs, logs2))
+    z_far = after(z_far, logs)
+    logs, ys2 = forward(some, (z_far,), olds=(logs,))
+    parcel = after(parcel, logs)
+    x2, z2 = call(
+        open_kernel, "open", (shape(dim, rows_own, dtype=bf16), shape(2, depth, cols_own, dtype=bf16)),
+        (core, parcel, after(swap(parcel), logs)), scalars=1,
+    )
     logs2 = forward((x2,), lefts=(ys0, ys1, ys2))[0]
-    over2 = swap(after(z2, logs))
-    over2 = after(over2, logs2)
-    logs = forward((*some, x2), (z2, over2), olds=(logs, logs2), mass=(mass_r,))[0]
+    logs = forward((*some, x2), (z2,), olds=(logs, logs2), mass=(mass_r,))[0]
 
     fars = [across(logs, "x", d) for d in (1, 3, 2)]
     potential, ready = call(
         merge_rows_kernel, "merge_rows",
         (shape(ring * row_lines, 128), shape(ring * rows_own, 128, dtype=jnp.bfloat16)),
-        (index_of("x"), logs, *fars, *some, x2), scalars=1,
+        (index_of("x"), core, logs, *fars, *some, x2), scalars=2,
     )
 
     block = ring * rows_own * cols_own
     other = call(
-        backward_kernel, "backward", shape(32, 128), (ready, over0, over1, over3, over2), pairs=4 * block,
-        scratch=[stack_of(4, cols_own)],
+        functools.partial(backward_kernel, 1), "backward", shape(32, 128),
+        (core, ready, over0, z_near, z_far, z2), pairs=4 * block, scratch=[stack_of(4, cols_own)], scalars=1,
     )
     to_core = call(to_core_kernel, "to_core", shape(56, 128), (other, potential))
     swapped = swap(to_core)
-    early = call(backward_kernel, "backward", shape(16, 128), (after(ready, to_core), own, z1), pairs=2 * block, scratch=[stack_of(2, cols_own)])
+    early = call(
+        functools.partial(backward_kernel, 0), "backward", shape(16, 128),
+        (core, after(ready, to_core), own, z_near), pairs=2 * block, scratch=[stack_of(2, cols_own)], scalars=1,
+    )
     swapped = after(swapped, early)
-    chip = call(pack_kernel, "pack", shape(48, 128), (index_of("k"), to_core, swapped), scalars=1)
+    chip = call(pack_kernel, "pack", shape(48, 128), (core, to_core, swapped), scalars=1)
     far = across(chip, "z", 3)
     sums = call(
         backward_last_kernel, "backward_last", shape(ring * ring, 8, 128),
-        (index_of("z"), ready, z3, z2, early, swapped),
-        pairs=2 * block, scratch=[pltpu.VMEM((16, 128), jnp.float32), stack_of(2, cols_own)], scalars=1,
+        (index_of("z"), core, ready, z_far, z2, early, swapped),
+        pairs=2 * block, scratch=[pltpu.VMEM((16, 128), jnp.float32), stack_of(2, cols_own)], scalars=2,
     )
     parts = lax.all_to_all(sums, ("y", "z"), 0, 0)
     chips = call(pack_two_kernel, "pack_two", shape(96, 128), (chip, after(far, sums)))

time: 252 us -> 249 us (0.988)
  starting transfers between devices: 27.6 us -> 23.2 us
  waiting for transfers between devices: 8.05 us -> 11.6 us
  local copies, waits for them, and re-layouts: 3.02 us -> 0.03 us
    ppermute x11 -> x5, starting transfers between devices: 20.1 us -> 6.55 us  [across(): return lax.ppermute(value, axis, [(i, i ^ bits) for i in range(ring)])]
    ppermute x0 -> x3, starting transfers between devices: none -> 5.45 us  [the longest x2 3.65 us: across_by_core(): return lax.ppermute(value, (axis, 'k'), pairs)]
    ppermute x5 -> x6, starting transfers between devices: 0.55 us -> 4.23 us  [swap(): return lax.ppermute(value, 'k', [(0, 1), (1, 0)])]
    unnamed x12 -> x10, local copies, waits for them, and re-layouts: 3.01 us -> 0.03 us
    ppermute x5 -> x6, waiting for transfers between devices: 0.01 us -> 2.67 us  [swap(): return lax.ppermute(value, 'k', [(0, 1), (1, 0)])]
    pallas_call x14 -> x20, Pallas kernels: 212 us -> 212 us  [call(): pl.pallas_call(kernel, out_shape=out, in_specs=specs, **within, scratch_s...]
  transfers between devices with their start and end apart: 17 -> 15, of which waited for: 3 -> 5; matrix products, arithmetic and copies ran while one was open for 0% -> 0% of each run, Pallas kernels for 62% -> 48%
where the time goes in v1:
time: 249 us
  Pallas kernels  214 us (86%)
  starting transfers between devices  23.2 us (9%)
  waiting for transfers between devices  11.6 us (5%)
    pallas_call x20, Pallas kernels, call(): pl.pallas_call(kernel, out_shape=out, in_specs=specs, **within, scratch_s...  212 us
    all_to_all x1, starting transfers between devices, body(): parts = lax.all_to_all(sums, ('y', 'z'), 0, 0)  6.95 us
    ppermute x5, starting transfers between devices, across(): return lax.ppermute(value, axis, [(i, i ^ bits) for i in range(ring)])  6.55 us
    all_to_all x1, waiting for transfers between devices, body(): parts = lax.all_to_all(sums, ('y', 'z'), 0, 0)  5.62 us
  transfers between devices with their start and end apart: 15, of which 5 were waited for; matrix products, arithmetic and copies ran while one was open for 0% of the time, Pallas kernels for 48%

profile of v1, /device:TPU:0, one launch (start us, length us, event | category | flops | bytes accessed | tf_op | source)
XLA Modules:
  0.0 249.2 jit_solution(16842869700203792361)
XLA Ops:
  0.6 0.1 collective-permute-start
  0.7 0.0 copy-start.1
  0.7 1.7 prepare.1.refs_1_.mine.refs_0_
  2.4 0.6 collective-permute-start.2
  3.0 0.0 collective-permute-done.theirs
  3.0 0.0 copy-done.1
  3.0 0.0 copy-start
  3.0 1.7 collective-permute-start.1
  4.7 0.0 collective-permute-done.2.refs_2_.theirs.refs_0_
  4.7 0.0 copy-done
  4.7 2.0 collective-permute-start.4
  6.7 12.5 %forward.6 = (f32[8,128]{1,0:T(8,128)S(1)}, bf16[2048,128]{1,0:T(8,128)(2,1)S(1)}) custom-call(bf16[64,768]{1,0:T(8,128)(2,1)S(1)} %bitcast.13, bf16[80,1024]{1,0:T(8,128)(2,1)S(1)} %copy-done, bf16[80,1024]{1,0:T(8,128)(2,1)S(1)} %collective-permute-done.2.refs_2_.theirs.refs_0_), custom_call_target="tpu_custom_call" | custom-call | flops 201326592 | bytes 1048576 | tf_op jit(solution)/shard_map/forward/pallas_call | solution.py:330
  19.3 0.0 collective-permute-done.1.pair.rows
  19.3 3.0 %collective-permute-start.3 = (bf16[2,64,768]{2,1,0:T(8,128)(2,1)S(1)}, bf16[2,64,768]{2,1,0:T(8,128)(2,1)S(1)}, u32[]{:S(2)}, u32[]{:S(2)}) collective-permute-start(bf16[2,64,768]{2,1,0:T(8,128)(2,1)S(1)} %collective-permute-done.1.pair.rows), channel_id=1, source_target_pairs={{0,1},{1,0},{2,3},{3,2},{4,5},{5,4},{6,7},{7,6},{8,9},{9,8},{10,11... | collective-permute-start | bytes 589832 | tf_op jit(solution)/shard_map/ppermute | solution.py:352
  22.2 1.1 collective-permute-done.3.pair
  23.3 24.3 %forward.7.refs_5_ = f32[16,128]{1,0:T(8,128)S(1)} custom-call(bf16[64,768]{1,0:T(8,128)(2,1)S(1)} %pick_near.1.refs_0_.refs_1_.x1, bf16[64,768]{1,0:T(8,128)(2,1)S(1)} %pick_far.1.refs_1_.refs_2_.x3, bf16[2048,128]{1,0:T(8,128)(2,1)S(1)} %get-tuple-element.24.refs_2_.refs_1_), custom_call_target="tpu_custom_call" | custom-call | flops 402653184 | bytes 1048576 | tf_op jit(solution)/shard_map/forward/pallas_call | solution.py:330
  47.6 0.0 collective-permute-done.4.cols.refs_3_.refs_1_
  47.6 0.5 collective-permute-start.6
  48.1 1.8 collective-permute-start.5
  49.9 36.8 %forward.8 = (f32[24,128]{1,0:T(8,128)S(1)}, bf16[2048,128]{1,0:T(8,128)(2,1)S(1)}) custom-call(bf16[64,768]{1,0:T(8,128)(2,1)S(1)} %bitcast.14, bf16[64,768]{1,0:T(8,128)(2,1)S(1)} %pick_near.1.refs_0_.refs_1_.x1, bf16[64,768]{1,0:T(8,128)(2,1)S(1)} %pick_far.1.refs_1_.refs_2_.x3, bf16[2,80,1024]{2,1,0:T(8,128)(2,1)S(1)} %collective-permute-done.4.cols.refs_3_.refs_1_, ...), custom_call_target="tpu_custom_call" | custom-call | flops 603979776 | bytes 1048576 | tf_op jit(solution)/shard_map/forward/pallas_call | solution.py:330
  86.7 0.0 collective-permute-done.6.refs_3_.refs_2_.c2
  86.7 0.0 copy-start.4
  86.7 36.8 %forward.9 = (f32[24,128]{1,0:T(8,128)S(1)}, bf16[2048,128]{1,0:T(8,128)(2,1)S(1)}) custom-call(bf16[64,768]{1,0:T(8,128)(2,1)S(1)} %bitcast.15, bf16[64,768]{1,0:T(8,128)(2,1)S(1)} %pick_near.1.refs_0_.refs_1_.x1, bf16[64,768]{1,0:T(8,128)(2,1)S(1)} %pick_far.1.refs_1_.refs_2_.x3, bf16[2,80,1024]{2,1,0:T(8,128)(2,1)S(1)} %collective-permute-done.6.refs_3_.refs_2_.c2, ...), custom_call_target="tpu_custom_call" | custom-call | flops 603979776 | bytes 1048576 | tf_op jit(solution)/shard_map/forward/pallas_call | solution.py:330
  123.6 0.0 collective-permute-done.5.here
  123.6 0.1 collective-permute-start.7
  123.7 0.0 copy-done.4
  123.7 1.6 collective-permute-done.7.there
  125.3 36.1 %forward.10.refs_6_ = f32[8,128]{1,0:T(8,128)S(1)} custom-call(bf16[64,768]{1,0:T(8,128)(2,1)S(1)} %get-tuple-element.31.refs_0_.refs_3_.x2, bf16[2048,128]{1,0:T(8,128)(2,1)S(1)} %get-tuple-element.24.refs_2_.refs_1_, bf16[2048,128]{1,0:T(8,128)(2,1)S(1)} %get-tuple-element.33.refs_2_, bf16[2048,128]{1,0:T(8,128)(2,1)S(1)} %get-tuple-element.34.refs_3_), custom_call_target="tpu_custom_call" | custom-call | flops 603979776 | bytes 1048576 | tf_op jit(solution)/shard_map/forward/pallas_call | solution.py:330
  161.4 48.6 %forward.11.own = f32[40,128]{1,0:T(8,128)S(1)} custom-call(bf16[64,768]{1,0:T(8,128)(2,1)S(1)} %bitcast.16, bf16[64,768]{1,0:T(8,128)(2,1)S(1)} %pick_near.1.refs_0_.refs_1_.x1, bf16[64,768]{1,0:T(8,128)(2,1)S(1)} %pick_far.1.refs_1_.refs_2_.x3, bf16[64,768]{1,0:T(8,128)(2,1)S(1)} %get-tuple-element.31.refs_0_.refs_3_.x2, ...), custom_call_target="tpu_custom_call" | custom-call | flops 805306368 | bytes 1048576 | tf_op jit(solution)/shard_map/forward/pallas_call | solution.py:330
  210.1 0.9 collective-permute-start.10
  211.0 1.6 collective-permute-start.8
  212.5 1.7 collective-permute-start.9
  214.2 1.2 collective-permute-done.10.far2
  215.4 0.0 collective-permute-done.8.far1
  215.4 2.1 collective-permute-done.9.far3
  217.5 0.3 merge_rows.1
  217.8 7.2 %backward.2.logs = f32[32,128]{1,0:T(8,128)S(1)} custom-call(s32[1]{0:T(128)} %bitcast.1.core, bf16[3072,128]{1,0:T(8,128)(2,1)S(1)} %get-tuple-element.37.xs, bf16[80,1024]{1,0:T(8,128)(2,1)S(1)} %collective-permute-done.2.refs_2_.theirs.refs_0_, bf16[2,80,1024]{2,1,0:T(8,128)(2,1)S(1)} %collective-permute-done.4.cols.refs_3_.refs_1_, ...), custom_call_target="tpu_custom_call" | custom-call | flops 6442450944 | bytes 1048576 | tf_op jit(solution)/shard_map/backward/pallas_call | solution.py:330
  225.1 0.1 collective-permute-start.11
  225.2 3.8 %backward.3.early = f32[16,128]{1,0:T(8,128)S(1)} custom-call(s32[1]{0:T(128)} %bitcast.1.core, bf16[3072,128]{1,0:T(8,128)(2,1)S(1)} %get-tuple-element.37.xs, bf16[80,1024]{1,0:T(8,128)(2,1)S(1)} %copy-done, bf16[2,80,1024]{2,1,0:T(8,128)(2,1)S(1)} %collective-permute-done.4.cols.refs_3_.refs_1_), custom_call_target="tpu_custom_call" | custom-call | flops 3221225472 | bytes 1048576 | tf_op jit(solution)/shard_map/backward/pallas_call | solution.py:330
  229.0 0.0 collective-permute-done.11.swapped.theirs
  229.1 0.4 collective-permute-start.12
  229.4 4.5 %backward_last.1 = f32[16,8,128]{2,1,0:T(8,128)} custom-call(s32[1]{0:T(128)} %bitcast.place_z, s32[1]{0:T(128)} %bitcast.1.core, bf16[3072,128]{1,0:T(8,128)(2,1)S(1)} %get-tuple-element.37.xs, bf16[2,80,1024]{2,1,0:T(8,128)(2,1)S(1)} %collective-permute-done.6.refs_3_.refs_2_.c2, bf16[2,80,1024]{2,1,0:T(8,128)(2,1)S(1)} %get-tuple-element.32.refs_4_.refs_3_.c3, ...), custom_call_target="tpu_custom_call" | custom-call | flops 3221225472 | bytes 1048576 | tf_op jit(solution)/shard_map/backward_last/pallas_call | solution.py:330
  233.9 7.0 %all-to-all-start = ((f32[16,8,128]{2,1,0:T(8,128)}), f32[16,8,128]{2,1,0:T(8,128)S(1)}, u32[]{:S(2)}, u32[]{:S(2)}) async-start(f32[16,8,128]{2,1,0:T(8,128)} %backward_last.1), calls=%async_computation | async-start | bytes 131072 | tf_op jit(solution)/shard_map/all_to_all | solution.py:470
  240.9 0.0 collective-permute-done.12.far
  240.9 0.0 copy-start.2
  240.9 0.0 copy-start.3
  240.9 2.0 collective-permute-start.13
  242.9 5.6 %all-to-all-done.parts = f32[16,8,128]{2,1,0:T(8,128)S(1)} async-done(((f32[16,8,128]{2,1,0:T(8,128)}), f32[16,8,128]{2,1,0:T(8,128)S(1)}, u32[]{:S(2)}, u32[]{:S(2)}) %all-to-all-start) | async-done | bytes 65568 | tf_op jit(solution)/shard_map/all_to_all | solution.py:470
  248.6 0.0 collective-permute-done.13.near
  248.6 0.0 copy-done.2
  248.6 0.0 copy-done.3
  248.6 0.7 finish.1
  (10 shorter events, 0.1 us)
Async XLA Ops:
  0.6 2.4 collective-permute-start
  0.7 2.3 copy-start.1
  2.4 2.3 collective-permute-start.2
  3.0 1.7 copy-start
  3.0 16.2 %collective-permute-start.1 = (bf16[2,64,768]{2,1,0:T(8,128)(2,1)S(1)}, bf16[2,64,768]{2,1,0:T(8,128)(2,1)S(1)}, u32[]{:S(2)}, u32[]{:S(2)}) collective-permute-start(bf16[2,64,768]{2,1,0:T(8,128)(2,1)S(1)} %pair_rows.1), channel_id=1, source_target_pairs={{0,2},{1,7},{2,0},{3,5},{4,6},{5,3},{6,4},{7,1},{8,10},{9,15},{10,... | collective-permute-start | bytes 589832 | tf_op jit(solution)/shard_map/ppermute | solution.py:348
  4.7 42.9 %collective-permute-start.4 = (bf16[2,80,1024]{2,1,0:T(8,128)(2,1)S(1)}, bf16[2,80,1024]{2,1,0:T(8,128)(2,1)S(1)}, u32[]{:S(2)}, u32[]{:S(2)}) collective-permute-start(bf16[2,80,1024]{2,1,0:T(8,128)(2,1)S(1)} %pair_cols.1), channel_id=1, source_target_pairs={{0,8},{1,25},{8,0},{9,17},{16,24},{17,9},{24,16},{25,1},{2,10},{3,... | collective-permute-start | bytes 983048 | tf_op jit(solution)/shard_map/ppermute | solution.py:348
  19.3 4.0 %collective-permute-start.3 = (bf16[2,64,768]{2,1,0:T(8,128)(2,1)S(1)}, bf16[2,64,768]{2,1,0:T(8,128)(2,1)S(1)}, u32[]{:S(2)}, u32[]{:S(2)}) collective-permute-start(bf16[2,64,768]{2,1,0:T(8,128)(2,1)S(1)} %collective-permute-done.1.pair.rows), channel_id=1, source_target_pairs={{0,1},{1,0},{2,3},{3,2},{4,5},{5,4},{6,7},{7,6},{8,9},{9,8},{10,11... | collective-permute-start | bytes 589832 | tf_op jit(solution)/shard_map/ppermute | solution.py:352
  47.6 39.1 %collective-permute-start.6 = (bf16[2,80,1024]{2,1,0:T(8,128)(2,1)S(1)}, bf16[2,80,1024]{2,1,0:T(8,128)(2,1)S(1)}, u32[]{:S(2)}, u32[]{:S(2)}) collective-permute-start(bf16[2,80,1024]{2,1,0:T(8,128)(2,1)S(1)} %collective-permute-done.4.cols.refs_3_.refs_1_), channel_id=1, source_target_pairs={{0,1},{1,0},{2,3},{3,2},{4,5},{5,4},{6,7},{7,6},{8,9},{9,8},{10,11... | collective-permute-start | bytes 983048 | tf_op jit(solution)/shard_map/ppermute | solution.py:352
  48.1 75.4 %collective-permute-start.5 = (bf16[2,80,1024]{2,1,0:T(8,128)(2,1)S(1)}, bf16[2,80,1024]{2,1,0:T(8,128)(2,1)S(1)}, u32[]{:S(2)}, u32[]{:S(2)}) collective-permute-start(bf16[2,80,1024]{2,1,0:T(8,128)(2,1)S(1)} %parcel.1), channel_id=1, source_target_pairs={{0,6},{1,9},{2,4},{3,11},{4,2},{5,13},{6,0},{7,15},{8,14},{9,1},{1... | collective-permute-start | bytes 983048 | tf_op jit(solution)/shard_map/ppermute | solution.py:427
  86.7 36.9 %copy-start.4 = (bf16[768]{0:T(1024)(128)(2,1)S(1)}, bf16[768]{0:T(1024)(128)(2,1)}, u32[]{:S(2)}) copy-start(bf16[768]{0:T(1024)(128)(2,1)} %param.7) | copy-start | bytes 4612
  123.6 1.7 collective-permute-start.7
  210.1 5.4 %collective-permute-start.10 = (f32[40,128]{1,0:T(8,128)S(1)}, f32[40,128]{1,0:T(8,128)S(1)}, u32[]{:S(2)}, u32[]{:S(2)}) collective-permute-start(f32[40,128]{1,0:T(8,128)S(1)} %forward.11.own), channel_id=1, source_target_pairs={{0,4},{2,6},{4,0},{6,2},{1,5},{3,7},{5,1},{7,3},{8,12},{10,14},{12... | collective-permute-start | bytes 61448 | tf_op jit(solution)/shard_map/ppermute | solution.py:343
  211.0 4.5 %collective-permute-start.8 = (f32[40,128]{1,0:T(8,128)S(1)}, f32[40,128]{1,0:T(8,128)S(1)}, u32[]{:S(2)}, u32[]{:S(2)}) collective-permute-start(f32[40,128]{1,0:T(8,128)S(1)} %forward.11.own), channel_id=1, source_target_pairs={{0,2},{2,0},{4,6},{6,4},{1,3},{3,1},{5,7},{7,5},{8,10},{10,8},{12,... | collective-permute-start | bytes 61448 | tf_op jit(solution)/shard_map/ppermute | solution.py:343
  212.5 5.0 %collective-permute-start.9 = (f32[40,128]{1,0:T(8,128)S(1)}, f32[40,128]{1,0:T(8,128)S(1)}, u32[]{:S(2)}, u32[]{:S(2)}) collective-permute-start(f32[40,128]{1,0:T(8,128)S(1)} %forward.11.own), channel_id=1, source_target_pairs={{0,6},{2,4},{4,2},{6,0},{1,7},{3,5},{5,3},{7,1},{8,14},{10,12},{12... | collective-permute-start | bytes 61448 | tf_op jit(solution)/shard_map/ppermute | solution.py:343
  225.1 3.9 %collective-permute-start.11 = (f32[56,128]{1,0:T(8,128)S(1)}, f32[56,128]{1,0:T(8,128)S(1)}, u32[]{:S(2)}, u32[]{:S(2)}) collective-permute-start(f32[56,128]{1,0:T(8,128)S(1)} %to_core.1.mine), channel_id=1, source_target_pairs={{0,1},{1,0},{2,3},{3,2},{4,5},{5,4},{6,7},{7,6},{8,9},{9,8},{10,11... | collective-permute-start | bytes 86024 | tf_op jit(solution)/shard_map/ppermute | solution.py:352
  229.1 11.8 %collective-permute-start.12 = (f32[48,128]{1,0:T(8,128)S(1)}, f32[48,128]{1,0:T(8,128)S(1)}, u32[]{:S(2)}, u32[]{:S(2)}) collective-permute-start(f32[48,128]{1,0:T(8,128)S(1)} %pack.1.mine), channel_id=1, source_target_pairs={{0,24},{8,16},{16,8},{24,0},{1,25},{9,17},{17,9},{25,1},{2,26},{10... | collective-permute-start | bytes 73736 | tf_op jit(solution)/shard_map/ppermute | solution.py:343
  233.9 14.6 %all-to-all-start = ((f32[16,8,128]{2,1,0:T(8,128)}), f32[16,8,128]{2,1,0:T(8,128)S(1)}, u32[]{:S(2)}, u32[]{:S(2)}) async-start(f32[16,8,128]{2,1,0:T(8,128)} %backward_last.1), calls=%async_computation | async-start | bytes 131072 | tf_op jit(solution)/shard_map/all_to_all | solution.py:470
  240.9 7.7 %copy-start.2 = (f32[1024]{0:T(1024)S(1)}, f32[1024]{0:T(1024)}, u32[]{:S(2)}) copy-start(f32[1024]{0:T(1024)} %param.9) | copy-start | bytes 12292
  240.9 7.7 %copy-start.3 = (f32[1024]{0:T(1024)S(1)}, f32[1024]{0:T(1024)}, u32[]{:S(2)}) copy-start(f32[1024]{0:T(1024)} %param.8) | copy-start | bytes 12292
  240.9 7.6 %collective-permute-start.13 = (f32[96,128]{1,0:T(8,128)S(1)}, f32[96,128]{1,0:T(8,128)S(1)}, u32[]{:S(2)}, u32[]{:S(2)}) collective-permute-start(f32[96,128]{1,0:T(8,128)S(1)} %pack_two.1.mine), channel_id=1, source_target_pairs={{0,8},{8,0},{16,24},{24,16},{1,9},{9,1},{17,25},{25,17},{2,10},{10... | collective-permute-start | bytes 147464 | tf_op jit(solution)/shard_map/ppermute | solution.py:343

commit v2 on v1

--- a/solution.py
+++ b/solution.py
@@ -180,7 +180,7 @@
                 ys[pl.ds(pl.multiple_of(q * cols_own + at, 128), 128), :] = turned(col[:, pl.ds(at, 128)])
                 return carry
 
-            lax.fori_loop(0, cols_own // 128, turn, 0, unroll=4)
+            lax.fori_loop(0, cols_own // 128, turn, 0, unroll=8)
         lefts = lefts + [ys]
     one = jnp.ones((1, rows_own), jnp.float32)
     extras = place([one, one, one], rows_own)
@@ -207,7 +207,7 @@
         return jnp.maximum(worst, logs)
 
     worst = jnp.full((1, rows_own), -finite_max, jnp.float32)
-    worst = lax.fori_loop(0, n_rows, block, worst, unroll=2 if n_rows == ring else 1)
+    worst = lax.fori_loop(0, n_rows, block, worst, unroll={1: 1, 2: 2, 3: 3, 4: 2}[n_rows])
 
     @pl.when(jnp.logical_not(jnp.max(worst) < finite_max))
     def _():
@@ -270,7 +270,7 @@
         return jnp.maximum(worst, found)
 
     worst = jnp.full((1, cols_own), -finite_max, jnp.float32)
-    worst = lax.fori_loop(0, len(cols), block, worst, unroll=2 if len(cols) > 2 else 1)
+    worst = lax.fori_loop(0, len(cols), block, worst, unroll=2)
 
     @pl.when(jnp.logical_not(jnp.max(worst) < finite_max))
     def _():

time: 249 us -> 248 us (level)
  Pallas kernels: 214 us -> 200 us
  starting transfers between devices: 23.2 us -> 33.9 us
    pallas_call x20, Pallas kernels: 212 us -> 199 us  [call(): pl.pallas_call(kernel, out_shape=out, in_specs=specs, **within, scratch_s...]
    ppermute x6, starting transfers between devices: 4.23 us -> 14.9 us  [swap(): return lax.ppermute(value, 'k', [(0, 1), (1, 0)])]
  transfers between devices with their start and end apart: 15 -> 15, of which waited for: 5 -> 6; matrix products, arithmetic and copies ran while one was open for 0% -> 0% of each run, Pallas kernels for 48% -> 44%
where the time goes in v2:
time: 248 us; the launch traced here: 247 us
  Pallas kernels  200 us (81%)
  starting transfers between devices  33.9 us (14%)
  waiting for transfers between devices  12.3 us (5%)
    pallas_call x20, Pallas kernels, call(): pl.pallas_call(kernel, out_shape=out, in_specs=specs, **within, scratch_s...  199 us
    ppermute x6, starting transfers between devices, swap(): return lax.ppermute(value, 'k', [(0, 1), (1, 0)])  14.9 us
    all_to_all x1, starting transfers between devices, body(): parts = lax.all_to_all(sums, ('y', 'z'), 0, 0)  6.95 us
    ppermute x5, starting transfers between devices, across(): return lax.ppermute(value, axis, [(i, i ^ bits) for i in range(ring)])  6.56 us
    all_to_all x1, waiting for transfers between devices, body(): parts = lax.all_to_all(sums, ('y', 'z'), 0, 0)  5.62 us
  transfers between devices with their start and end apart: 15, of which 6 were waited for; matrix products, arithmetic and copies ran while one was open for 0% of the time, Pallas kernels for 44%

profile of v2, /device:TPU:0, one launch (start us, length us, event | category | flops | bytes accessed | tf_op | source)
XLA Modules:
  0.0 247.4 jit_solution(9103371512952137721)
XLA Ops:
  0.6 0.1 collective-permute-start
  0.7 0.0 copy-start.1
  0.7 1.7 prepare.1.refs_1_.mine.refs_0_
  2.4 0.6 collective-permute-start.2
  3.0 0.0 collective-permute-done.theirs
  3.0 0.0 copy-done.1
  3.0 0.0 copy-start
  3.0 1.7 collective-permute-start.1
  4.7 0.0 collective-permute-done.2.refs_2_.theirs.refs_0_
  4.7 0.0 copy-done
  4.7 2.0 collective-permute-start.4
  6.7 1.3 forward.6
  8.1 0.7 collective-permute-done.1.pair.rows
  8.8 13.4 %collective-permute-start.3 = (bf16[2,64,768]{2,1,0:T(8,128)(2,1)S(1)}, bf16[2,64,768]{2,1,0:T(8,128)(2,1)S(1)}, u32[]{:S(2)}, u32[]{:S(2)}) collective-permute-start(bf16[2,64,768]{2,1,0:T(8,128)(2,1)S(1)} %collective-permute-done.1.pair.rows), channel_id=1, source_target_pairs={{0,1},{1,0},{2,3},{3,2},{4,5},{5,4},{6,7},{7,6},{8,9},{9,8},{10,11... | collective-permute-start | bytes 589832 | tf_op jit(solution)/shard_map/ppermute | solution.py:352
  22.2 1.1 collective-permute-done.3.pair
  23.3 24.1 %forward.7.refs_5_ = f32[16,128]{1,0:T(8,128)S(1)} custom-call(bf16[64,768]{1,0:T(8,128)(2,1)S(1)} %pick_near.1.refs_0_.refs_1_.x1, bf16[64,768]{1,0:T(8,128)(2,1)S(1)} %pick_far.1.refs_1_.refs_2_.x3, bf16[2048,128]{1,0:T(8,128)(2,1)S(1)} %get-tuple-element.24.refs_2_.refs_1_), custom_call_target="tpu_custom_call" | custom-call | flops 402653184 | bytes 1048576 | tf_op jit(solution)/shard_map/forward/pallas_call | solution.py:330
  47.4 0.0 collective-permute-done.4.cols.refs_3_.refs_1_
  47.4 0.5 collective-permute-start.6
  47.9 1.8 collective-permute-start.5
  49.7 36.2 %forward.8 = (f32[24,128]{1,0:T(8,128)S(1)}, bf16[2048,128]{1,0:T(8,128)(2,1)S(1)}) custom-call(bf16[64,768]{1,0:T(8,128)(2,1)S(1)} %bitcast.14, bf16[64,768]{1,0:T(8,128)(2,1)S(1)} %pick_near.1.refs_0_.refs_1_.x1, bf16[64,768]{1,0:T(8,128)(2,1)S(1)} %pick_far.1.refs_1_.refs_2_.x3, bf16[2,80,1024]{2,1,0:T(8,128)(2,1)S(1)} %collective-permute-done.4.cols.refs_3_.refs_1_, ...), custom_call_target="tpu_custom_call" | custom-call | flops 603979776 | bytes 1048576 | tf_op jit(solution)/shard_map/forward/pallas_call | solution.py:330
  85.9 0.0 collective-permute-done.6.refs_3_.refs_2_.c2
  85.9 0.0 copy-start.4
  85.9 36.3 %forward.9 = (f32[24,128]{1,0:T(8,128)S(1)}, bf16[2048,128]{1,0:T(8,128)(2,1)S(1)}) custom-call(bf16[64,768]{1,0:T(8,128)(2,1)S(1)} %bitcast.15, bf16[64,768]{1,0:T(8,128)(2,1)S(1)} %pick_near.1.refs_0_.refs_1_.x1, bf16[64,768]{1,0:T(8,128)(2,1)S(1)} %pick_far.1.refs_1_.refs_2_.x3, bf16[2,80,1024]{2,1,0:T(8,128)(2,1)S(1)} %collective-permute-done.6.refs_3_.refs_2_.c2, ...), custom_call_target="tpu_custom_call" | custom-call | flops 603979776 | bytes 1048576 | tf_op jit(solution)/shard_map/forward/pallas_call | solution.py:330
  122.2 0.0 collective-permute-done.5.here
  122.3 0.1 collective-permute-start.7
  122.3 0.0 copy-done.4
  122.4 1.6 collective-permute-done.7.there
  124.0 0.2 open.1
  124.2 35.9 %forward.10.refs_6_ = f32[8,128]{1,0:T(8,128)S(1)} custom-call(bf16[64,768]{1,0:T(8,128)(2,1)S(1)} %get-tuple-element.31.refs_0_.refs_3_.x2, bf16[2048,128]{1,0:T(8,128)(2,1)S(1)} %get-tuple-element.24.refs_2_.refs_1_, bf16[2048,128]{1,0:T(8,128)(2,1)S(1)} %get-tuple-element.33.refs_2_, bf16[2048,128]{1,0:T(8,128)(2,1)S(1)} %get-tuple-element.34.refs_3_), custom_call_target="tpu_custom_call" | custom-call | flops 603979776 | bytes 1048576 | tf_op jit(solution)/shard_map/forward/pallas_call | solution.py:330
  160.1 48.3 %forward.11.own = f32[40,128]{1,0:T(8,128)S(1)} custom-call(bf16[64,768]{1,0:T(8,128)(2,1)S(1)} %bitcast.16, bf16[64,768]{1,0:T(8,128)(2,1)S(1)} %pick_near.1.refs_0_.refs_1_.x1, bf16[64,768]{1,0:T(8,128)(2,1)S(1)} %pick_far.1.refs_1_.refs_2_.x3, bf16[64,768]{1,0:T(8,128)(2,1)S(1)} %get-tuple-element.31.refs_0_.refs_3_.x2, ...), custom_call_target="tpu_custom_call" | custom-call | flops 805306368 | bytes 1048576 | tf_op jit(solution)/shard_map/forward/pallas_call | solution.py:330
  208.4 0.9 collective-permute-start.10
  209.3 1.6 collective-permute-start.8
  210.8 1.7 collective-permute-start.9
  212.6 1.2 collective-permute-done.10.far2
  213.8 0.0 collective-permute-done.8.far1
  213.8 2.1 collective-permute-done.9.far3
  215.8 0.3 merge_rows.1
  216.1 7.2 %backward.2.logs = f32[32,128]{1,0:T(8,128)S(1)} custom-call(s32[1]{0:T(128)} %bitcast.1.core, bf16[3072,128]{1,0:T(8,128)(2,1)S(1)} %get-tuple-element.37.xs, bf16[80,1024]{1,0:T(8,128)(2,1)S(1)} %collective-permute-done.2.refs_2_.theirs.refs_0_, bf16[2,80,1024]{2,1,0:T(8,128)(2,1)S(1)} %collective-permute-done.4.cols.refs_3_.refs_1_, ...), custom_call_target="tpu_custom_call" | custom-call | flops 6442450944 | bytes 1048576 | tf_op jit(solution)/shard_map/backward/pallas_call | solution.py:330
  223.4 0.3 collective-permute-start.11
  223.7 3.7 %backward.3.early = f32[16,128]{1,0:T(8,128)S(1)} custom-call(s32[1]{0:T(128)} %bitcast.1.core, bf16[3072,128]{1,0:T(8,128)(2,1)S(1)} %get-tuple-element.37.xs, bf16[80,1024]{1,0:T(8,128)(2,1)S(1)} %copy-done, bf16[2,80,1024]{2,1,0:T(8,128)(2,1)S(1)} %collective-permute-done.4.cols.refs_3_.refs_1_), custom_call_target="tpu_custom_call" | custom-call | flops 3221225472 | bytes 1048576 | tf_op jit(solution)/shard_map/backward/pallas_call | solution.py:330
  227.4 0.0 collective-permute-done.11.swapped.theirs
  227.4 0.4 collective-permute-start.12
  227.8 4.3 %backward_last.1 = f32[16,8,128]{2,1,0:T(8,128)} custom-call(s32[1]{0:T(128)} %bitcast.place_z, s32[1]{0:T(128)} %bitcast.1.core, bf16[3072,128]{1,0:T(8,128)(2,1)S(1)} %get-tuple-element.37.xs, bf16[2,80,1024]{2,1,0:T(8,128)(2,1)S(1)} %collective-permute-done.6.refs_3_.refs_2_.c2, bf16[2,80,1024]{2,1,0:T(8,128)(2,1)S(1)} %get-tuple-element.32.refs_4_.refs_3_.c3, ...), custom_call_target="tpu_custom_call" | custom-call | flops 3221225472 | bytes 1048576 | tf_op jit(solution)/shard_map/backward_last/pallas_call | solution.py:330
  232.1 6.9 %all-to-all-start = ((f32[16,8,128]{2,1,0:T(8,128)}), f32[16,8,128]{2,1,0:T(8,128)S(1)}, u32[]{:S(2)}, u32[]{:S(2)}) async-start(f32[16,8,128]{2,1,0:T(8,128)} %backward_last.1), calls=%async_computation | async-start | bytes 131072 | tf_op jit(solution)/shard_map/all_to_all | solution.py:470
  239.1 0.0 collective-permute-done.12.far
  239.1 0.0 copy-start.2
  239.1 0.0 copy-start.3
  239.1 2.0 collective-permute-start.13
  241.1 5.6 %all-to-all-done.parts = f32[16,8,128]{2,1,0:T(8,128)S(1)} async-done(((f32[16,8,128]{2,1,0:T(8,128)}), f32[16,8,128]{2,1,0:T(8,128)S(1)}, u32[]{:S(2)}, u32[]{:S(2)}) %all-to-all-start) | async-done | bytes 65568 | tf_op jit(solution)/shard_map/all_to_all | solution.py:470
  246.7 0.0 collective-permute-done.13.near
  246.7 0.0 copy-done.2
  246.7 0.0 copy-done.3
  246.7 0.7 finish.1
  (9 shorter events, 0.1 us)
Async XLA Ops:
  0.6 2.4 collective-permute-start
  0.7 2.3 copy-start.1
  2.4 2.3 collective-permute-start.2
  3.0 1.7 copy-start
  3.0 5.7 %collective-permute-start.1 = (bf16[2,64,768]{2,1,0:T(8,128)(2,1)S(1)}, bf16[2,64,768]{2,1,0:T(8,128)(2,1)S(1)}, u32[]{:S(2)}, u32[]{:S(2)}) collective-permute-start(bf16[2,64,768]{2,1,0:T(8,128)(2,1)S(1)} %pair_rows.1), channel_id=1, source_target_pairs={{0,2},{1,7},{2,0},{3,5},{4,6},{5,3},{6,4},{7,1},{8,10},{9,15},{10,... | collective-permute-start | bytes 589832 | tf_op jit(solution)/shard_map/ppermute | solution.py:348
  4.7 42.7 %collective-permute-start.4 = (bf16[2,80,1024]{2,1,0:T(8,128)(2,1)S(1)}, bf16[2,80,1024]{2,1,0:T(8,128)(2,1)S(1)}, u32[]{:S(2)}, u32[]{:S(2)}) collective-permute-start(bf16[2,80,1024]{2,1,0:T(8,128)(2,1)S(1)} %pair_cols.1), channel_id=1, source_target_pairs={{0,8},{1,25},{8,0},{9,17},{16,24},{17,9},{24,16},{25,1},{2,10},{3,... | collective-permute-start | bytes 983048 | tf_op jit(solution)/shard_map/ppermute | solution.py:348
  8.8 14.5 %collective-permute-start.3 = (bf16[2,64,768]{2,1,0:T(8,128)(2,1)S(1)}, bf16[2,64,768]{2,1,0:T(8,128)(2,1)S(1)}, u32[]{:S(2)}, u32[]{:S(2)}) collective-permute-start(bf16[2,64,768]{2,1,0:T(8,128)(2,1)S(1)} %collective-permute-done.1.pair.rows), channel_id=1, source_target_pairs={{0,1},{1,0},{2,3},{3,2},{4,5},{5,4},{6,7},{7,6},{8,9},{9,8},{10,11... | collective-permute-start | bytes 589832 | tf_op jit(solution)/shard_map/ppermute | solution.py:352
  47.4 38.5 %collective-permute-start.6 = (bf16[2,80,1024]{2,1,0:T(8,128)(2,1)S(1)}, bf16[2,80,1024]{2,1,0:T(8,128)(2,1)S(1)}, u32[]{:S(2)}, u32[]{:S(2)}) collective-permute-start(bf16[2,80,1024]{2,1,0:T(8,128)(2,1)S(1)} %collective-permute-done.4.cols.refs_3_.refs_1_), channel_id=1, source_target_pairs={{0,1},{1,0},{2,3},{3,2},{4,5},{5,4},{6,7},{7,6},{8,9},{9,8},{10,11... | collective-permute-start | bytes 983048 | tf_op jit(solution)/shard_map/ppermute | solution.py:352
  47.9 74.4 %collective-permute-start.5 = (bf16[2,80,1024]{2,1,0:T(8,128)(2,1)S(1)}, bf16[2,80,1024]{2,1,0:T(8,128)(2,1)S(1)}, u32[]{:S(2)}, u32[]{:S(2)}) collective-permute-start(bf16[2,80,1024]{2,1,0:T(8,128)(2,1)S(1)} %parcel.1), channel_id=1, source_target_pairs={{0,6},{1,9},{2,4},{3,11},{4,2},{5,13},{6,0},{7,15},{8,14},{9,1},{1... | collective-permute-start | bytes 983048 | tf_op jit(solution)/shard_map/ppermute | solution.py:427
  85.9 36.4 %copy-start.4 = (bf16[768]{0:T(1024)(128)(2,1)S(1)}, bf16[768]{0:T(1024)(128)(2,1)}, u32[]{:S(2)}) copy-start(bf16[768]{0:T(1024)(128)(2,1)} %param.7) | copy-start | bytes 4612
  122.3 1.7 collective-permute-start.7
  208.4 5.4 %collective-permute-start.10 = (f32[40,128]{1,0:T(8,128)S(1)}, f32[40,128]{1,0:T(8,128)S(1)}, u32[]{:S(2)}, u32[]{:S(2)}) collective-permute-start(f32[40,128]{1,0:T(8,128)S(1)} %forward.11.own), channel_id=1, source_target_pairs={{0,4},{2,6},{4,0},{6,2},{1,5},{3,7},{5,1},{7,3},{8,12},{10,14},{12... | collective-permute-start | bytes 61448 | tf_op jit(solution)/shard_map/ppermute | solution.py:343
  209.3 4.5 %collective-permute-start.8 = (f32[40,128]{1,0:T(8,128)S(1)}, f32[40,128]{1,0:T(8,128)S(1)}, u32[]{:S(2)}, u32[]{:S(2)}) collective-permute-start(f32[40,128]{1,0:T(8,128)S(1)} %forward.11.own), channel_id=1, source_target_pairs={{0,2},{2,0},{4,6},{6,4},{1,3},{3,1},{5,7},{7,5},{8,10},{10,8},{12,... | collective-permute-start | bytes 61448 | tf_op jit(solution)/shard_map/ppermute | solution.py:343
  210.8 5.0 %collective-permute-start.9 = (f32[40,128]{1,0:T(8,128)S(1)}, f32[40,128]{1,0:T(8,128)S(1)}, u32[]{:S(2)}, u32[]{:S(2)}) collective-permute-start(f32[40,128]{1,0:T(8,128)S(1)} %forward.11.own), channel_id=1, source_target_pairs={{0,6},{2,4},{4,2},{6,0},{1,7},{3,5},{5,3},{7,1},{8,14},{10,12},{12... | collective-permute-start | bytes 61448 | tf_op jit(solution)/shard_map/ppermute | solution.py:343
  223.4 4.0 %collective-permute-start.11 = (f32[56,128]{1,0:T(8,128)S(1)}, f32[56,128]{1,0:T(8,128)S(1)}, u32[]{:S(2)}, u32[]{:S(2)}) collective-permute-start(f32[56,128]{1,0:T(8,128)S(1)} %to_core.1.mine), channel_id=1, source_target_pairs={{0,1},{1,0},{2,3},{3,2},{4,5},{5,4},{6,7},{7,6},{8,9},{9,8},{10,11... | collective-permute-start | bytes 86024 | tf_op jit(solution)/shard_map/ppermute | solution.py:352
  227.4 11.7 %collective-permute-start.12 = (f32[48,128]{1,0:T(8,128)S(1)}, f32[48,128]{1,0:T(8,128)S(1)}, u32[]{:S(2)}, u32[]{:S(2)}) collective-permute-start(f32[48,128]{1,0:T(8,128)S(1)} %pack.1.mine), channel_id=1, source_target_pairs={{0,24},{8,16},{16,8},{24,0},{1,25},{9,17},{17,9},{25,1},{2,26},{10... | collective-permute-start | bytes 73736 | tf_op jit(solution)/shard_map/ppermute | solution.py:343
  232.1 14.6 %all-to-all-start = ((f32[16,8,128]{2,1,0:T(8,128)}), f32[16,8,128]{2,1,0:T(8,128)S(1)}, u32[]{:S(2)}, u32[]{:S(2)}) async-start(f32[16,8,128]{2,1,0:T(8,128)} %backward_last.1), calls=%async_computation | async-start | bytes 131072 | tf_op jit(solution)/shard_map/all_to_all | solution.py:470
  239.1 7.7 %copy-start.2 = (f32[1024]{0:T(1024)S(1)}, f32[1024]{0:T(1024)}, u32[]{:S(2)}) copy-start(f32[1024]{0:T(1024)} %param.9) | copy-start | bytes 12292
  239.1 7.7 %copy-start.3 = (f32[1024]{0:T(1024)S(1)}, f32[1024]{0:T(1024)}, u32[]{:S(2)}) copy-start(f32[1024]{0:T(1024)} %param.8) | copy-start | bytes 12292
  239.1 7.6 %collective-permute-start.13 = (f32[96,128]{1,0:T(8,128)S(1)}, f32[96,128]{1,0:T(8,128)S(1)}, u32[]{:S(2)}, u32[]{:S(2)}) collective-permute-start(f32[96,128]{1,0:T(8,128)S(1)} %pack_two.1.mine), channel_id=1, source_target_pairs={{0,8},{8,0},{16,24},{24,16},{1,9},{9,1},{17,25},{25,17},{2,10},{10... | collective-permute-start | bytes 147464 | tf_op jit(solution)/shard_map/ppermute | solution.py:343

commit v3 on v2

--- a/solution.py
+++ b/solution.py
@@ -416,8 +416,10 @@
     x_near = after(x_near, logs)
     x_far = swap(x_near)
     x1 = pick("pick_near", x_near)
+    logs1 = forward((x1,), lefts=(ys0,))[0]
+    x_far = after(x_far, logs1)
     x3 = pick("pick_far", x_far)
-    logs2 = forward((x1, x3), lefts=(ys0,))[0]
+    logs2 = forward((x3,), lefts=(ys0,))[0]
     z_near = after(z_near, logs2)
     parcel = call(
         parcel_kernel, "parcel", shape(2, depth, cols_own, dtype=bf16), (core, x_near, z_near), scalars=1
@@ -430,7 +432,7 @@
     )
     z_far = swap(z_near)
     some = (mine, x1, x3)
-    logs, ys1 = forward(some, (z_near,), olds=(logs, logs2))
+    logs, ys1 = forward(some, (z_near,), olds=(logs, logs1, logs2))
     z_far = after(z_far, logs)
     logs, ys2 = forward(some, (z_far,), olds=(logs,))
     parcel = after(parcel, logs)

time: 248 us -> 246 us (level)
  Pallas kernels: 200 us -> 212 us
  starting transfers between devices: 33.9 us -> 23.1 us
    pallas_call x20 -> x21, Pallas kernels: 199 us -> 210 us  [call(): pl.pallas_call(kernel, out_shape=out, in_specs=specs, **within, scratch_s...]
    ppermute x6, starting transfers between devices: 14.9 us -> 4.1 us  [swap(): return lax.ppermute(value, 'k', [(0, 1), (1, 0)])]
  transfers between devices with their start and end apart: 15 -> 15, of which waited for: 6 -> 4; matrix products, arithmetic and copies ran while one was open for 0% -> 0% of each run, Pallas kernels for 44% -> 48%
where the time goes in v3:
time: 246 us
  Pallas kernels  212 us (86%)
  starting transfers between devices  23.1 us (9%)
  waiting for transfers between devices  10.5 us (4%)
    pallas_call x21, Pallas kernels, call(): pl.pallas_call(kernel, out_shape=out, in_specs=specs, **within, scratch_s...  210 us
    all_to_all x1, starting transfers between devices, body(): parts = lax.all_to_all(sums, ('y', 'z'), 0, 0)  6.95 us
    ppermute x5, starting transfers between devices, across(): return lax.ppermute(value, axis, [(i, i ^ bits) for i in range(ring)])  6.56 us
    all_to_all x1, waiting for transfers between devices, body(): parts = lax.all_to_all(sums, ('y', 'z'), 0, 0)  5.62 us
  transfers between devices with their start and end apart: 15, of which 4 were waited for; matrix products, arithmetic and copies ran while one was open for 0% of the time, Pallas kernels for 48%

profile of v3, /device:TPU:0, one launch (start us, length us, event | category | flops | bytes accessed | tf_op | source)
XLA Modules:
  0.0 246.3 jit_solution(17380756564188018420)
XLA Ops:
  0.6 0.1 collective-permute-start
  0.7 0.0 copy-start.1
  0.7 1.7 prepare.1.refs_1_.mine.refs_0_
  2.4 0.6 collective-permute-start.2
  3.0 0.0 collective-permute-done.theirs
  3.0 0.0 copy-done.1
  3.0 0.0 copy-start
  3.0 1.7 collective-permute-start.1
  4.7 0.0 collective-permute-done.2.refs_2_.theirs.refs_0_
  4.7 0.0 copy-done
  4.7 2.0 collective-permute-start.4
  6.7 12.5 %forward.7 = (f32[8,128]{1,0:T(8,128)S(1)}, bf16[2048,128]{1,0:T(8,128)(2,1)S(1)}) custom-call(bf16[64,768]{1,0:T(8,128)(2,1)S(1)} %bitcast.13, bf16[80,1024]{1,0:T(8,128)(2,1)S(1)} %copy-done, bf16[80,1024]{1,0:T(8,128)(2,1)S(1)} %collective-permute-done.2.refs_2_.theirs.refs_0_), custom_call_target="tpu_custom_call" | custom-call | flops 201326592 | bytes 1048576 | tf_op jit(solution)/shard_map/forward/pallas_call | solution.py:330
  19.3 0.0 collective-permute-done.1.pair.rows
  19.3 2.9 %collective-permute-start.3 = (bf16[2,64,768]{2,1,0:T(8,128)(2,1)S(1)}, bf16[2,64,768]{2,1,0:T(8,128)(2,1)S(1)}, u32[]{:S(2)}, u32[]{:S(2)}) collective-permute-start(bf16[2,64,768]{2,1,0:T(8,128)(2,1)S(1)} %collective-permute-done.1.pair.rows), channel_id=1, source_target_pairs={{0,1},{1,0},{2,3},{3,2},{4,5},{5,4},{6,7},{7,6},{8,9},{9,8},{10,11... | collective-permute-start | bytes 589832 | tf_op jit(solution)/shard_map/ppermute | solution.py:352
  22.2 12.2 %forward.8.refs_5_ = f32[8,128]{1,0:T(8,128)S(1)} custom-call(bf16[64,768]{1,0:T(8,128)(2,1)S(1)} %pick_near.1.refs_0_.refs_1_.x1, bf16[2048,128]{1,0:T(8,128)(2,1)S(1)} %get-tuple-element.25.refs_1_), custom_call_target="tpu_custom_call" | custom-call | flops 201326592 | bytes 1048576 | tf_op jit(solution)/shard_map/forward/pallas_call | solution.py:330
  34.4 0.0 collective-permute-done.3.pair
  34.4 12.2 %forward.9.refs_6_ = f32[8,128]{1,0:T(8,128)S(1)} custom-call(bf16[64,768]{1,0:T(8,128)(2,1)S(1)} %pick_far.1.refs_0_.refs_2_.x3, bf16[2048,128]{1,0:T(8,128)(2,1)S(1)} %get-tuple-element.25.refs_1_), custom_call_target="tpu_custom_call" | custom-call | flops 201326592 | bytes 1048576 | tf_op jit(solution)/shard_map/forward/pallas_call | solution.py:330
  46.6 0.0 collective-permute-done.4.cols.refs_3_.refs_1_
  46.6 0.1 collective-permute-start.6
  46.8 1.8 collective-permute-start.5
  48.6 36.2 %forward.10 = (f32[24,128]{1,0:T(8,128)S(1)}, bf16[2048,128]{1,0:T(8,128)(2,1)S(1)}) custom-call(bf16[64,768]{1,0:T(8,128)(2,1)S(1)} %bitcast.14, bf16[64,768]{1,0:T(8,128)(2,1)S(1)} %pick_near.1.refs_0_.refs_1_.x1, bf16[64,768]{1,0:T(8,128)(2,1)S(1)} %pick_far.1.refs_0_.refs_2_.x3, bf16[2,80,1024]{2,1,0:T(8,128)(2,1)S(1)} %collective-permute-done.4.cols.refs_3_.refs_1_, ...), custom_call_target="tpu_custom_call" | custom-call | flops 603979776 | bytes 1048576 | tf_op jit(solution)/shard_map/forward/pallas_call | solution.py:330
  84.8 0.0 collective-permute-done.6.refs_3_.refs_2_.c2
  84.8 0.0 copy-start.4
  84.8 36.3 %forward.11 = (f32[24,128]{1,0:T(8,128)S(1)}, bf16[2048,128]{1,0:T(8,128)(2,1)S(1)}) custom-call(bf16[64,768]{1,0:T(8,128)(2,1)S(1)} %bitcast.15, bf16[64,768]{1,0:T(8,128)(2,1)S(1)} %pick_near.1.refs_0_.refs_1_.x1, bf16[64,768]{1,0:T(8,128)(2,1)S(1)} %pick_far.1.refs_0_.refs_2_.x3, bf16[2,80,1024]{2,1,0:T(8,128)(2,1)S(1)} %collective-permute-done.6.refs_3_.refs_2_.c2, ...), custom_call_target="tpu_custom_call" | custom-call | flops 603979776 | bytes 1048576 | tf_op jit(solution)/shard_map/forward/pallas_call | solution.py:330
  121.1 0.0 collective-permute-done.5.here
  121.1 0.1 collective-permute-start.7
  121.2 0.0 copy-done.4
  121.3 1.6 collective-permute-done.7.there
  122.8 0.2 open.1
  123.1 35.9 %forward.12.refs_6_ = f32[8,128]{1,0:T(8,128)S(1)} custom-call(bf16[64,768]{1,0:T(8,128)(2,1)S(1)} %get-tuple-element.33.refs_0_.refs_3_.x2, bf16[2048,128]{1,0:T(8,128)(2,1)S(1)} %get-tuple-element.25.refs_1_, bf16[2048,128]{1,0:T(8,128)(2,1)S(1)} %get-tuple-element.35.refs_2_, bf16[2048,128]{1,0:T(8,128)(2,1)S(1)} %get-tuple-element.36.refs_3_), custom_call_target="tpu_custom_call" | custom-call | flops 603979776 | bytes 1048576 | tf_op jit(solution)/shard_map/forward/pallas_call | solution.py:330
  159.0 48.3 %forward.13.own = f32[40,128]{1,0:T(8,128)S(1)} custom-call(bf16[64,768]{1,0:T(8,128)(2,1)S(1)} %bitcast.16, bf16[64,768]{1,0:T(8,128)(2,1)S(1)} %pick_near.1.refs_0_.refs_1_.x1, bf16[64,768]{1,0:T(8,128)(2,1)S(1)} %pick_far.1.refs_0_.refs_2_.x3, bf16[64,768]{1,0:T(8,128)(2,1)S(1)} %get-tuple-element.33.refs_0_.refs_3_.x2, ...), custom_call_target="tpu_custom_call" | custom-call | flops 805306368 | bytes 1048576 | tf_op jit(solution)/shard_map/forward/pallas_call | solution.py:330
  207.3 0.9 collective-permute-start.10
  208.2 1.6 collective-permute-start.8
  209.7 1.7 collective-permute-start.9
  211.5 1.2 collective-permute-done.10.far2
  212.6 0.0 collective-permute-done.8.far1
  212.6 2.1 collective-permute-done.9.far3
  214.7 0.3 merge_rows.1
  215.0 7.2 %backward.2.logs = f32[32,128]{1,0:T(8,128)S(1)} custom-call(s32[1]{0:T(128)} %bitcast.1.core, bf16[3072,128]{1,0:T(8,128)(2,1)S(1)} %get-tuple-element.39.xs, bf16[80,1024]{1,0:T(8,128)(2,1)S(1)} %collective-permute-done.2.refs_2_.theirs.refs_0_, bf16[2,80,1024]{2,1,0:T(8,128)(2,1)S(1)} %collective-permute-done.4.cols.refs_3_.refs_1_, ...), custom_call_target="tpu_custom_call" | custom-call | flops 6442450944 | bytes 1048576 | tf_op jit(solution)/shard_map/backward/pallas_call | solution.py:330
  222.3 0.3 collective-permute-start.11
  222.6 3.7 %backward.3.early = f32[16,128]{1,0:T(8,128)S(1)} custom-call(s32[1]{0:T(128)} %bitcast.1.core, bf16[3072,128]{1,0:T(8,128)(2,1)S(1)} %get-tuple-element.39.xs, bf16[80,1024]{1,0:T(8,128)(2,1)S(1)} %copy-done, bf16[2,80,1024]{2,1,0:T(8,128)(2,1)S(1)} %collective-permute-done.4.cols.refs_3_.refs_1_), custom_call_target="tpu_custom_call" | custom-call | flops 3221225472 | bytes 1048576 | tf_op jit(solution)/shard_map/backward/pallas_call | solution.py:330
  226.3 0.0 collective-permute-done.11.swapped.theirs
  226.3 0.4 collective-permute-start.12
  226.7 4.3 %backward_last.1 = f32[16,8,128]{2,1,0:T(8,128)} custom-call(s32[1]{0:T(128)} %bitcast.place_z, s32[1]{0:T(128)} %bitcast.1.core, bf16[3072,128]{1,0:T(8,128)(2,1)S(1)} %get-tuple-element.39.xs, bf16[2,80,1024]{2,1,0:T(8,128)(2,1)S(1)} %collective-permute-done.6.refs_3_.refs_2_.c2, bf16[2,80,1024]{2,1,0:T(8,128)(2,1)S(1)} %get-tuple-element.34.refs_4_.refs_3_.c3, ...), custom_call_target="tpu_custom_call" | custom-call | flops 3221225472 | bytes 1048576 | tf_op jit(solution)/shard_map/backward_last/pallas_call | solution.py:330
  231.0 6.9 %all-to-all-start = ((f32[16,8,128]{2,1,0:T(8,128)}), f32[16,8,128]{2,1,0:T(8,128)S(1)}, u32[]{:S(2)}, u32[]{:S(2)}) async-start(f32[16,8,128]{2,1,0:T(8,128)} %backward_last.1), calls=%async_computation | async-start | bytes 131072 | tf_op jit(solution)/shard_map/all_to_all | solution.py:472
  238.0 0.0 collective-permute-done.12.far
  238.0 0.0 copy-start.2
  238.0 0.0 copy-start.3
  238.0 2.0 collective-permute-start.13
  240.0 5.6 %all-to-all-done.parts = f32[16,8,128]{2,1,0:T(8,128)S(1)} async-done(((f32[16,8,128]{2,1,0:T(8,128)}), f32[16,8,128]{2,1,0:T(8,128)S(1)}, u32[]{:S(2)}, u32[]{:S(2)}) %all-to-all-start) | async-done | bytes 65568 | tf_op jit(solution)/shard_map/all_to_all | solution.py:472
  245.6 0.0 collective-permute-done.13.near
  245.6 0.0 copy-done.2
  245.6 0.0 copy-done.3
  245.6 0.7 finish.1
  (9 shorter events, 0.1 us)
Async XLA Ops:
  0.6 2.4 collective-permute-start
  0.7 2.3 copy-start.1
  2.4 2.3 collective-permute-start.2
  3.0 1.7 copy-start
  3.0 16.2 %collective-permute-start.1 = (bf16[2,64,768]{2,1,0:T(8,128)(2,1)S(1)}, bf16[2,64,768]{2,1,0:T(8,128)(2,1)S(1)}, u32[]{:S(2)}, u32[]{:S(2)}) collective-permute-start(bf16[2,64,768]{2,1,0:T(8,128)(2,1)S(1)} %pair_rows.1), channel_id=1, source_target_pairs={{0,2},{1,7},{2,0},{3,5},{4,6},{5,3},{6,4},{7,1},{8,10},{9,15},{10,... | collective-permute-start | bytes 589832 | tf_op jit(solution)/shard_map/ppermute | solution.py:348
  4.7 41.9 %collective-permute-start.4 = (bf16[2,80,1024]{2,1,0:T(8,128)(2,1)S(1)}, bf16[2,80,1024]{2,1,0:T(8,128)(2,1)S(1)}, u32[]{:S(2)}, u32[]{:S(2)}) collective-permute-start(bf16[2,80,1024]{2,1,0:T(8,128)(2,1)S(1)} %pair_cols.1), channel_id=1, source_target_pairs={{0,8},{1,25},{8,0},{9,17},{16,24},{17,9},{24,16},{25,1},{2,10},{3,... | collective-permute-start | bytes 983048 | tf_op jit(solution)/shard_map/ppermute | solution.py:348
  19.3 15.1 %collective-permute-start.3 = (bf16[2,64,768]{2,1,0:T(8,128)(2,1)S(1)}, bf16[2,64,768]{2,1,0:T(8,128)(2,1)S(1)}, u32[]{:S(2)}, u32[]{:S(2)}) collective-permute-start(bf16[2,64,768]{2,1,0:T(8,128)(2,1)S(1)} %collective-permute-done.1.pair.rows), channel_id=1, source_target_pairs={{0,1},{1,0},{2,3},{3,2},{4,5},{5,4},{6,7},{7,6},{8,9},{9,8},{10,11... | collective-permute-start | bytes 589832 | tf_op jit(solution)/shard_map/ppermute | solution.py:352
  46.6 38.2 %collective-permute-start.6 = (bf16[2,80,1024]{2,1,0:T(8,128)(2,1)S(1)}, bf16[2,80,1024]{2,1,0:T(8,128)(2,1)S(1)}, u32[]{:S(2)}, u32[]{:S(2)}) collective-permute-start(bf16[2,80,1024]{2,1,0:T(8,128)(2,1)S(1)} %collective-permute-done.4.cols.refs_3_.refs_1_), channel_id=1, source_target_pairs={{0,1},{1,0},{2,3},{3,2},{4,5},{5,4},{6,7},{7,6},{8,9},{9,8},{10,11... | collective-permute-start | bytes 983048 | tf_op jit(solution)/shard_map/ppermute | solution.py:352
  46.8 74.4 %collective-permute-start.5 = (bf16[2,80,1024]{2,1,0:T(8,128)(2,1)S(1)}, bf16[2,80,1024]{2,1,0:T(8,128)(2,1)S(1)}, u32[]{:S(2)}, u32[]{:S(2)}) collective-permute-start(bf16[2,80,1024]{2,1,0:T(8,128)(2,1)S(1)} %parcel.1), channel_id=1, source_target_pairs={{0,6},{1,9},{2,4},{3,11},{4,2},{5,13},{6,0},{7,15},{8,14},{9,1},{1... | collective-permute-start | bytes 983048 | tf_op jit(solution)/shard_map/ppermute | solution.py:429
  84.8 36.4 %copy-start.4 = (bf16[768]{0:T(1024)(128)(2,1)S(1)}, bf16[768]{0:T(1024)(128)(2,1)}, u32[]{:S(2)}) copy-start(bf16[768]{0:T(1024)(128)(2,1)} %param.7) | copy-start | bytes 4612
  121.1 1.7 collective-permute-start.7
  207.3 5.4 %collective-permute-start.10 = (f32[40,128]{1,0:T(8,128)S(1)}, f32[40,128]{1,0:T(8,128)S(1)}, u32[]{:S(2)}, u32[]{:S(2)}) collective-permute-start(f32[40,128]{1,0:T(8,128)S(1)} %forward.13.own), channel_id=1, source_target_pairs={{0,4},{2,6},{4,0},{6,2},{1,5},{3,7},{5,1},{7,3},{8,12},{10,14},{12... | collective-permute-start | bytes 61448 | tf_op jit(solution)/shard_map/ppermute | solution.py:343
  208.2 4.5 %collective-permute-start.8 = (f32[40,128]{1,0:T(8,128)S(1)}, f32[40,128]{1,0:T(8,128)S(1)}, u32[]{:S(2)}, u32[]{:S(2)}) collective-permute-start(f32[40,128]{1,0:T(8,128)S(1)} %forward.13.own), channel_id=1, source_target_pairs={{0,2},{2,0},{4,6},{6,4},{1,3},{3,1},{5,7},{7,5},{8,10},{10,8},{12,... | collective-permute-start | bytes 61448 | tf_op jit(solution)/shard_map/ppermute | solution.py:343
  209.7 5.0 %collective-permute-start.9 = (f32[40,128]{1,0:T(8,128)S(1)}, f32[40,128]{1,0:T(8,128)S(1)}, u32[]{:S(2)}, u32[]{:S(2)}) collective-permute-start(f32[40,128]{1,0:T(8,128)S(1)} %forward.13.own), channel_id=1, source_target_pairs={{0,6},{2,4},{4,2},{6,0},{1,7},{3,5},{5,3},{7,1},{8,14},{10,12},{12... | collective-permute-start | bytes 61448 | tf_op jit(solution)/shard_map/ppermute | solution.py:343
  222.3 4.0 %collective-permute-start.11 = (f32[56,128]{1,0:T(8,128)S(1)}, f32[56,128]{1,0:T(8,128)S(1)}, u32[]{:S(2)}, u32[]{:S(2)}) collective-permute-start(f32[56,128]{1,0:T(8,128)S(1)} %to_core.1.mine), channel_id=1, source_target_pairs={{0,1},{1,0},{2,3},{3,2},{4,5},{5,4},{6,7},{7,6},{8,9},{9,8},{10,11... | collective-permute-start | bytes 86024 | tf_op jit(solution)/shard_map/ppermute | solution.py:352
  226.3 11.7 %collective-permute-start.12 = (f32[48,128]{1,0:T(8,128)S(1)}, f32[48,128]{1,0:T(8,128)S(1)}, u32[]{:S(2)}, u32[]{:S(2)}) collective-permute-start(f32[48,128]{1,0:T(8,128)S(1)} %pack.1.mine), channel_id=1, source_target_pairs={{0,24},{8,16},{16,8},{24,0},{1,25},{9,17},{17,9},{25,1},{2,26},{10... | collective-permute-start | bytes 73736 | tf_op jit(solution)/shard_map/ppermute | solution.py:343
  231.0 14.6 %all-to-all-start = ((f32[16,8,128]{2,1,0:T(8,128)}), f32[16,8,128]{2,1,0:T(8,128)S(1)}, u32[]{:S(2)}, u32[]{:S(2)}) async-start(f32[16,8,128]{2,1,0:T(8,128)} %backward_last.1), calls=%async_computation | async-start | bytes 131072 | tf_op jit(solution)/shard_map/all_to_all | solution.py:472
  238.0 7.7 %copy-start.2 = (f32[1024]{0:T(1024)S(1)}, f32[1024]{0:T(1024)}, u32[]{:S(2)}) copy-start(f32[1024]{0:T(1024)} %param.9) | copy-start | bytes 12292
  238.0 7.7 %copy-start.3 = (f32[1024]{0:T(1024)S(1)}, f32[1024]{0:T(1024)}, u32[]{:S(2)}) copy-start(f32[1024]{0:T(1024)} %param.8) | copy-start | bytes 12292
  238.0 7.6 %collective-permute-start.13 = (f32[96,128]{1,0:T(8,128)S(1)}, f32[96,128]{1,0:T(8,128)S(1)}, u32[]{:S(2)}, u32[]{:S(2)}) collective-permute-start(f32[96,128]{1,0:T(8,128)S(1)} %pack_two.1.mine), channel_id=1, source_target_pairs={{0,8},{8,0},{16,24},{24,16},{1,9},{9,1},{17,25},{25,17},{2,10},{10... | collective-permute-start | bytes 147464 | tf_op jit(solution)/shard_map/ppermute | solution.py:343
